TPU v7x, 256 devices: a whole 4x4x8 slice. The times are simulated.
256 devices in a mesh: star: 2 (over x_hi), blk: 128 (over x_lo, y, z, core).
Axes of the slice: x: 4 (x_hi: 2, x_lo: 2; x = x_hi * 2 + x_lo), y: 4, z: 8, core: 2. Of those that a mesh axis runs over, the one named last changes fastest.
Arguments:
- lapse_field: float32 [2048, 16, 256], P(('star', 'blk')), may hold values from 0.3 to 1
- conformal: float32 [2048, 16, 256], P(('star', 'blk')), may hold values from 0.5 to 1.5
- mean_curv: float32 [2048, 16, 256], P(('star', 'blk')), may hold values from -3 to 3
- conformal_metric: float32 [6, 2048, 16, 256], P(None, ('star', 'blk')), may hold values from -0.3 to 1.6, as said below
- traceless_curv: float32 [6, 2048, 16, 256], P(None, ('star', 'blk')), may hold values from -2 to 2
- shift_vector: float32 [3, 2048, 16, 256], P(None, ('star', 'blk')), may hold values from -3 to 3
- density: float32 [2, 2048, 16, 256], P('star', 'blk'), may hold values from 0.2 to 2
- momentum: float32 [2, 3, 2048, 16, 256], P('star', None, 'blk'), may hold values from -3 to 3
- energy: float32 [2, 2048, 16, 256], P('star', 'blk'), may hold values from 0.2 to 2
- velocity: float32 [2, 3, 2048, 16, 256], P('star', None, 'blk'), may hold values from -0.5 to 0.5
- pressure: float32 [2, 2048, 16, 256], P('star', 'blk'), may hold values from 0.05 to 0.5
Outputs:
- bssn_rhs: float32 [15, 2048, 16, 256], P(None, ('star', 'blk'))
- hydro_rhs: float32 [2, 5, 2048, 16, 256], P('star', None, 'blk')
Inputs may be any that keep to these rules, and one draw needn't show every extreme that they name: `conformal_metric`: in every cell the symmetric matrix with rows (xx, xy, xz), (xy, yy, yz), (xz, yz, zz) has diagonal entries from 0.8 to 1.6 and off-diagonal entries from -0.3 to 0.3, and each diagonal entry exceeds the sum of the magnitudes of the other entries of its row.
All inputs are finite; a program needn't handle non-finite values.
Results may differ from a plain program's by a relative error of at most 0.0003.
Values sent between devices are 32-bit elements; how exact they have to be, the bound alone decides.
A program may use at most 128 MiB of HBM per device.

v0:
```python
from functools import reduce
import math

import jax
import jax.numpy as jnp
from jax import lax
from jax.sharding import PartitionSpec as P

pair_index = ((0, 1, 2), (1, 3, 4), (2, 4, 5))
sym_pairs = ((0, 0), (0, 1), (0, 2), (1, 1), (1, 2), (2, 2))
weno_eps = 1e-06


def extended(array, sides, width):
    edges = {}
    for axis, dim in sides:
        count, length = (lax.axis_size(axis), array.shape[dim])
        up = [(i, (i + 1) % count) for i in range(count)]
        last = lax.slice_in_dim(array, length - width, length, axis=dim)
        leading = lax.slice_in_dim(array, 0, width, axis=dim)
        edges[dim] = (
            lax.ppermute(last, axis, up),
            lax.ppermute(leading, axis, [(b, a) for a, b in up]),
        )
    done = []
    for _, dim in sides:
        low, high = edges[dim]
        around = [(width, width) if d in done else (0, 0) for d in range(array.ndim)]
        array = jnp.concatenate([jnp.pad(low, around), array, jnp.pad(high, around)], axis=dim)
        done.append(dim)
    return array


def passed_along(value, axis, steps):
    count = lax.axis_size(axis)
    pairs = [(source, (source + steps) % count) for source in range(count)]
    return lax.ppermute(value, axis, pairs)


def from_behind(array, axis, by):
    count = lax.axis_size(axis)
    pairs = [(i, i + by) for i in range(count) if 0 <= i + by < count]
    return lax.ppermute(array, axis, pairs)


def extended_2(array, sides, width):
    for axis, dim in sides:
        count, length = (lax.axis_size(axis), array.shape[dim])
        up = [(i, (i + 1) % count) for i in range(count - 1)]
        down = [(j, i) for i, j in up]
        last = lax.slice_in_dim(array, length - width, length, axis=dim)
        leading = lax.slice_in_dim(array, 0, width, axis=dim)
        before = lax.ppermute(last, axis, up)
        after = lax.ppermute(leading, axis, down)
        array = jnp.concatenate([before, array, after], axis=dim)
    return array


def accumulate(terms):
    return reduce(lambda x, y: x + y, terms)


def xfirst(values):
    return (
        values[..., 0:-4, :, :]
        - 8.0 * values[..., 1:-3, :, :]
        + 8.0 * values[..., 3:-1, :, :]
        - values[..., 4:, :, :]
    ) / 12.0


def xsecond(values):
    return (
        -values[..., 0:-4, :, :]
        + 16.0 * values[..., 1:-3, :, :]
        - 30.0 * values[..., 2:-2, :, :]
        + 16.0 * values[..., 3:-1, :, :]
        - values[..., 4:, :, :]
    ) / 12.0


def rfirst(values, direction):
    return (
        jnp.roll(values, 2, direction)
        - 8.0 * jnp.roll(values, 1, direction)
        + 8.0 * jnp.roll(values, -1, direction)
        - jnp.roll(values, -2, direction)
    ) / 12.0


def rsecond(values, direction):
    return (
        -jnp.roll(values, 2, direction)
        + 16.0 * jnp.roll(values, 1, direction)
        - 30.0 * values
        + 16.0 * jnp.roll(values, -1, direction)
        - jnp.roll(values, -2, direction)
    ) / 12.0


def bssn_rates(padded, sources):
    core_cells = padded[:, 2:-2]
    gradients = (xfirst(padded), rfirst(core_cells, -2), rfirst(core_cells, -1))
    lapse_core = core_cells[0]
    conf_core = core_cells[1]
    mean_core = core_cells[2]
    shift_core = core_cells[15:18]
    advected = (
        shift_core[0] * gradients[0][:15]
        + shift_core[1] * gradients[1][:15]
        + shift_core[2] * gradients[2][:15]
    )

    def metric_at(i, j):
        return core_cells[3 + pair_index[i][j]]

    def curv_at(i, j):
        return core_cells[9 + pair_index[i][j]]

    def dshift(k, i):
        return gradients[k][15 + i]

    div_shift = dshift(0, 0) + dshift(1, 1) + dshift(2, 2)
    a, b, c, d, e, f = [core_cells[3 + n] for n in range(6)]
    cofactor = (
        d * f - e * e,
        c * e - b * f,
        b * e - c * d,
        a * f - c * c,
        b * c - a * e,
        a * d - b * b,
    )
    determ = a * cofactor[0] + b * cofactor[1] + c * cofactor[2]
    inverse = [entry / determ for entry in cofactor]

    def inverse_at(i, j):
        return inverse[pair_index[i][j]]

    lapse_pad = padded[0]
    hessian = (
        xsecond(lapse_pad),
        xfirst(rfirst(lapse_pad, -2)),
        xfirst(rfirst(lapse_pad, -1)),
        rsecond(lapse_core, -2),
        rfirst(rfirst(lapse_core, -1), -2),
        rsecond(lapse_core, -1),
    )

    def hess_at(i, j):
        return hessian[pair_index[i][j]]

    trace_hess = accumulate([inverse_at(i, j) * hess_at(i, j) for i in range(3) for j in range(3)])
    mixed_curv = [
        [accumulate([curv_at(i, l) * inverse_at(l, j) for l in range(3)]) for j in range(3)]
        for i in range(3)
    ]
    square_trace = accumulate(
        [mixed_curv[i][j] * mixed_curv[j][i] for i in range(3) for j in range(3)]
    )
    lapse_rate = advected[0] - 2.0 * lapse_core * mean_core
    conf_rate = advected[1] + 2.0 / 3.0 * conf_core * (lapse_core * mean_core - div_shift)
    mean_rate = (
        advected[2]
        - conf_core * trace_hess
        + lapse_core * (square_trace + mean_core * mean_core / 3.0)
        + 4.0 * math.pi * lapse_core * sources[0]
    )
    metric_rates = []
    curv_rates = []
    for p, (i, j) in enumerate(sym_pairs):
        moved_metric = accumulate(
            [metric_at(i, k) * dshift(j, k) + metric_at(j, k) * dshift(i, k) for k in range(3)]
        )
        metric_rates.append(
            advected[3 + p]
            - 2.0 * lapse_core * curv_at(i, j)
            + moved_metric
            - 2.0 / 3.0 * metric_at(i, j) * div_shift
        )
        moved_curv = accumulate(
            [curv_at(i, k) * dshift(j, k) + curv_at(j, k) * dshift(i, k) for k in range(3)]
        )
        product = accumulate([mixed_curv[i][k] * curv_at(k, j) for k in range(3)])
        curv_rates.append(
            advected[9 + p]
            + lapse_core * (mean_core * curv_at(i, j) - 2.0 * product)
            + moved_curv
            - 2.0 / 3.0 * curv_at(i, j) * div_shift
            - conf_core * (hess_at(i, j) - trace_hess * metric_at(i, j) / 3.0)
        )
    return jnp.stack([lapse_rate, conf_rate, mean_rate] + metric_rates + curv_rates, 0)


def restrict(fine_cells):
    leading = fine_cells.shape[:-3]
    extent_x, extent_y, extent_z = fine_cells.shape[-3:]
    blocks = fine_cells.reshape(leading + (extent_x // 2, 2, extent_y // 2, 2, extent_z // 2, 2))
    return jnp.sum(blocks, axis=(-5, -3, -1)) * 0.125


def refine_axis(coarse, axis_index):
    cell_count = coarse.shape[axis_index] - 2
    center = lax.slice_in_dim(coarse, 1, cell_count + 1, axis=axis_index)
    lower_side = lax.slice_in_dim(coarse, 0, cell_count, axis=axis_index)
    upper_side = lax.slice_in_dim(coarse, 2, cell_count + 2, axis=axis_index)
    even_cells = 0.75 * center + 0.25 * lower_side
    odd_cells = 0.75 * center + 0.25 * upper_side
    stacked = jnp.stack([even_cells, odd_cells], axis_index + 1)
    new_shape = coarse.shape[:axis_index] + (2 * cell_count,) + coarse.shape[axis_index + 1 :]
    return stacked.reshape(new_shape)


def prolong(window):
    return refine_axis(refine_axis(refine_axis(window, 1), 2), 3)


def split_fluxes(conserved, velocity, pressure, fine_metric):
    lapse_fine = fine_metric[0]
    shift_fine = fine_metric[1]
    conf_fine = fine_metric[2]
    transport = lapse_fine * velocity[0] - shift_fine
    weight = lapse_fine * conf_fine ** (-1.5) * pressure
    flux_terms = jnp.stack(
        [
            conserved[0] * transport,
            conserved[1] * transport + weight,
            conserved[2] * transport,
            conserved[3] * transport,
            conserved[4] * transport + weight * velocity[0],
        ],
        0,
    )
    max_speed = lapse_fine + jnp.abs(shift_fine)
    return jnp.concatenate(
        [0.5 * (flux_terms + max_speed * conserved), 0.5 * (flux_terms - max_speed * conserved)], 0
    )


def weno_value(left_two, left_one, middle, right_one, right_two):
    guess_one = (2.0 * left_two - 7.0 * left_one + 11.0 * middle) / 6.0
    guess_two = (-left_one + 5.0 * middle + 2.0 * right_one) / 6.0
    guess_three = (2.0 * middle + 5.0 * right_one - right_two) / 6.0
    smooth_one = (
        13.0 / 12.0 * (left_two - 2.0 * left_one + middle) ** 2
        + 0.25 * (left_two - 4.0 * left_one + 3.0 * middle) ** 2
    )
    smooth_two = (
        13.0 / 12.0 * (left_one - 2.0 * middle + right_one) ** 2
        + 0.25 * (left_one - right_one) ** 2
    )
    smooth_three = (
        13.0 / 12.0 * (middle - 2.0 * right_one + right_two) ** 2
        + 0.25 * (3.0 * middle - 4.0 * right_one + right_two) ** 2
    )
    weight_one = 0.1 / (weno_eps + smooth_one) ** 2
    weight_two = 0.6 / (weno_eps + smooth_two) ** 2
    weight_three = 0.3 / (weno_eps + smooth_three) ** 2
    return (weight_one * guess_one + weight_two * guess_two + weight_three * guess_three) / (
        weight_one + weight_two + weight_three
    )


def weno_rates(ghosts):
    cell_count = ghosts.shape[1] - 6
    plus_part = ghosts[:5]
    minus_part = ghosts[5:]

    def taps(values, start):
        return values[:, start : start + cell_count + 1]

    face_flux = weno_value(
        taps(plus_part, 0),
        taps(plus_part, 1),
        taps(plus_part, 2),
        taps(plus_part, 3),
        taps(plus_part, 4),
    ) + weno_value(
        taps(minus_part, 5),
        taps(minus_part, 4),
        taps(minus_part, 3),
        taps(minus_part, 2),
        taps(minus_part, 1),
    )
    return (face_flux[:, :-1] - face_flux[:, 1:]) * 2.0


def on_device(
    lapse_field,
    conformal,
    mean_curv,
    conformal_metric,
    traceless_curv,
    shift_vector,
    density,
    momentum,
    energy,
    velocity,
    pressure,
):
    metric_state = jnp.concatenate(
        [
            lapse_field[None],
            conformal[None],
            mean_curv[None],
            conformal_metric,
            traceless_curv,
            shift_vector,
        ],
        0,
    )
    extent_x = lapse_field.shape[0]
    extent_y = lapse_field.shape[1]
    extent_z = lapse_field.shape[2]
    conserved = jnp.concatenate([density[:, None], momentum, energy[:, None]], 1)[0]
    source_fine = (
        energy
        + density
        + (
            momentum[:, 0] * velocity[:, 0]
            + momentum[:, 1] * velocity[:, 1]
            + momentum[:, 2] * velocity[:, 2]
        )
        + 3.0 * pressure
    )
    source_coarse = restrict(source_fine)
    footprint = ((0, 0), (0, 0), (extent_y // 4, extent_y // 4), (extent_z // 4, extent_z // 4))
    padded = extended(metric_state, ((("star", "blk"), 1),), 2)
    upper_plane = passed_along(source_coarse[:, extent_x - 1 :], ("star", "blk"), 1)
    sources = jnp.pad(
        jnp.concatenate([upper_plane, source_coarse[:, : extent_x - 1]], 1), footprint
    )
    bssn_rhs = bssn_rates(padded, sources)
    window = jnp.stack([padded[0], padded[15], padded[1]], 0)
    window = window[
        :, :, extent_y // 4 - 1 : 3 * extent_y // 4 + 1, extent_z // 4 - 1 : 3 * extent_z // 4 + 1
    ]
    upper_layers = from_behind(window[:, 4:6], ("star", "blk"), -1)
    coarse_wide = jnp.concatenate([window, upper_layers], 1)
    fine_wide = prolong(coarse_wide)[:, 1 : 2 * extent_x + 7]
    fluid = jnp.concatenate([conserved, velocity[0, :1], pressure], 0)
    fluid_wide = extended_2(fluid, (("blk", 1),), 3)
    ghosts = split_fluxes(fluid_wide[:5], fluid_wide[5:6], fluid_wide[6], fine_wide)
    hydro_rhs = weno_rates(ghosts)[None]
    return (bssn_rhs, hydro_rhs)


def solution(mesh):
    in_specs = (
        P(("star", "blk"), None, None),
        P(("star", "blk"), None, None),
        P(("star", "blk"), None, None),
        P(None, ("star", "blk"), None, None),
        P(None, ("star", "blk"), None, None),
        P(None, ("star", "blk"), None, None),
        P("star", "blk", None, None),
        P("star", None, "blk", None, None),
        P("star", "blk", None, None),
        P("star", None, "blk", None, None),
        P("star", "blk", None, None),
    )
    out_specs = (P(None, ("star", "blk"), None, None), P("star", None, "blk", None, None))
    return jax.shard_map(
        on_device, mesh=mesh, in_specs=in_specs, out_specs=out_specs, check_vma=False
    )
```

profile of v0, /device:TPU:6, one launch (start us, length us, event | category | flops | bytes accessed | tf_op | source)
XLA Modules:
  0.0 135.7 jit_solution(12712521717591329981)
XLA Ops:
  0.7 1.0 bitcast_dynamic-update-slice_fusion.2
  1.7 0.9 bitcast_dynamic-update-slice_fusion.1
  2.6 0.9 bitcast_dynamic-update-slice_fusion
  3.5 1.2 constant_dynamic-update-slice_fusion.2
  4.9 1.1 fusion.312
  6.0 8.0 %collective-permute-start.1 = (f32[18,2,16,256]{3,2,1,0:T(8,128)}, f32[18,2,16,256]{3,2,1,0:T(8,128)}, u32[]{:S(2)}, u32[]{:S(2)}) collective-permute-start(f32[18,2,16,256]{3,2,1,0:T(8,128)} %get-tuple-element.41), channel_id=1, source_target_pairs={{1,0},{2,1},{3,2},{4,3},{5,4},{6,5},{7,6},{8,7},{9,8},{10,9},{11,1... | collective-permute-start | bytes 1769480 | tf_op jit(solution)/shard_map/ppermute | solution.py:23
  14.1 1.0 fusion.44
  15.0 18.8 %reshape.109 = f32[8,2,8,2,128,2]{5,4,3,2,1,0:T(8,128)} reshape(f32[1,16,16,256]{3,2,1,0:T(8,128)} %fusion.44) | data formatting | bytes 524288 | tf_op jit(solution)/shard_map/reshape | solution.py:197
  33.9 7.0 %reduce_sum.9 = f32[8,8,128]{2,1,0:T(8,128)S(1)} reduce(f32[8,2,8,2,128,2]{5,4,3,2,1,0:T(8,128)} %reshape.109, f32[]{:T(128)} %constant.35.clone.1), dimensions={1,3,5}, to_apply=%region_0.0 | reduce | flops 57344 | bytes 294916 | tf_op jit(solution)/shard_map/reduce_sum | solution.py:198
  40.9 0.6 slice.1017
  41.5 1.0 slice_bitcast_fusion
  42.5 1.5 %maximum_bitcast_fusion = f32[5,16,16,256]{3,2,1,0:T(8,128)S(1)} fusion(f32[1,1,16,16,256]{4,3,2,1,0:T(8,128)} %bitcast.1211, f32[1,3,16,16,256]{4,3,2,1,0:T(8,128)} %param.18, f32[1,1,16,16,256]{4,3,2,1,0:T(8,128)} %bitcast.1212), kind=kLoop, calls=%fused_computation.47 | loop fusion | flops 655360 | bytes 2621440 | tf_op jit(solution)/shard_map/squeeze | solution.py:314
  44.0 0.9 pad_maximum_fusion.7
  44.9 7.9 %collective-permute-start.4 = (f32[7,3,16,256]{3,2,1,0:T(8,128)}, f32[7,3,16,256]{3,2,1,0:T(8,128)}, u32[]{:S(2)}, u32[]{:S(2)}) collective-permute-start(f32[7,3,16,256]{3,2,1,0:T(8,128)} %get-tuple-element.59), channel_id=1, source_target_pairs={{1,0},{2,1},{3,2},{4,3},{5,4},{6,5},{7,6},{8,7},{9,8},{10,9},{11,1... | collective-permute-start | bytes 1032200 | tf_op jit(solution)/shard_map/ppermute | solution.py:54
  52.7 2.1 %collective-permute-start.3 = (f32[7,3,16,256]{3,2,1,0:T(8,128)}, f32[7,3,16,256]{3,2,1,0:T(8,128)}, u32[]{:S(2)}, u32[]{:S(2)}) collective-permute-start(f32[7,3,16,256]{3,2,1,0:T(8,128)} %get-tuple-element.58), channel_id=1, source_target_pairs={{0,1},{1,2},{2,3},{3,4},{4,5},{5,6},{6,7},{7,8},{8,9},{9,10},{10,1... | collective-permute-start | bytes 1032200 | tf_op jit(solution)/shard_map/ppermute | solution.py:53
  54.8 0.6 fusion.313
  55.4 1.1 fusion.314
  56.6 0.6 fusion.315
  57.1 0.9 fusion.316
  58.1 1.8 %fusion.318 = (f32[18,8,16,2]{3,2,1,0:T(8,128)}, f32[18,8,16,2]{3,2,1,0:T(8,128)}) fusion(f32[18,8,16,256]{3,2,1,0:T(8,128)S(1)} %constant_dynamic-update-slice_fusion), kind=kLoop, calls=%fused_computation.568 | loop fusion | bytes 73728 | tf_op jit(solution)/shard_map/jit(_roll_static)/slice | solution.py:87
  59.9 2.3 %fusion.317 = (f32[18,8,16,254]{3,2,1,0:T(8,128)S(1)}, f32[18,8,16,254]{3,2,1,0:T(8,128)}) fusion(f32[18,8,16,256]{3,2,1,0:T(8,128)S(1)} %constant_dynamic-update-slice_fusion), kind=kLoop, calls=%fused_computation.567 | loop fusion | bytes 9363456 | tf_op jit(solution)/shard_map/jit(_roll_static)/slice | solution.py:87
  62.2 1.9 %fusion.320 = (f32[18,8,16,1]{3,2,1,0:T(8,128)}, f32[18,8,16,1]{3,2,1,0:T(8,128)}) fusion(f32[18,8,16,256]{3,2,1,0:T(8,128)S(1)} %constant_dynamic-update-slice_fusion), kind=kLoop, calls=%fused_computation.570 | loop fusion | bytes 36864 | tf_op jit(solution)/shard_map/jit(_roll_static)/slice | solution.py:86
  64.1 3.0 %fusion.319 = (f32[18,8,16,255]{3,2,1,0:T(8,128)}, f32[18,8,16,255]{3,2,1,0:T(8,128)}) fusion(f32[18,8,16,256]{3,2,1,0:T(8,128)S(1)} %constant_dynamic-update-slice_fusion), kind=kLoop, calls=%fused_computation.569 | loop fusion | bytes 9400320 | tf_op jit(solution)/shard_map/jit(_roll_static)/slice | solution.py:86
  67.2 0.8 slice_bitcast_fusion.27
  68.0 0.8 fusion.292
  69.3 0.6 fusion.329
  70.0 0.8 fusion.330
  70.8 0.8 fusion.341
  71.6 7.0 %fusion.12 = (f32[18,8,16,256]{3,2,1,0:T(8,128)S(1)}, f32[18,8,16,256]{3,2,1,0:T(8,128)S(1)}) fusion(f32[18,8,14,256]{3,2,1,0:T(8,128)S(1)} %get-tuple-element.43, f32[18,8,2,256]{3,2,1,0:T(2,128)} %get-tuple-element.45, f32[18,8,15,256]{3,2,1,0:T(8,128)S(1)} %get-tuple-element.47, f32[18,8,1,256]{3,2,1,0:T(1,128)} %get-tuple-element.49, ...), kind=kLoop, calls=%fused_computation.26 | loop fusion | flops 11796480 | bytes 23592960 | tf_op jit(solution)/shard_map/div | solution.py:83
  78.7 3.0 %pad_maximum_fusion = f32[7,22,16,256]{3,2,1,0:T(8,128)} fusion(f32[7,3,16,256]{3,2,1,0:T(8,128)} %collective-permute-done.4, f32[1,16,16,256]{3,2,1,0:T(8,128)S(1)} %copy-done.7, f32[1,16,16,256]{3,2,1,0:T(8,128)} %copy-done.8, f32[5,16,16,256]{3,2,1,0:T(8,128)S(1)} %maximum_bitcast_fusion, f32[7,3,16,256]{3,2,1,0:T(8,128)} %collective-permute-done.3), kind=kLoop, calls=%fused_computation.12 | loop fusion | flops 2523136 | bytes 5046272 | tf_op jit(solution)/shard_map/concatenate | solution.py:55
  81.7 0.8 pad_maximum_fusion.8
  82.5 0.8 fusion.45
  83.9 2.4 %fusion.4 = f32[18,8,16,256]{3,2,1,0:T(8,128)S(1)} fusion(f32[18,8,16,256]{3,2,1,0:T(8,128)S(1)} %constant_dynamic-update-slice_fusion, f32[18,2,16,256]{3,2,1,0:T(8,128)} %collective-permute-done.1, f32[18,2,16,256]{3,2,1,0:T(8,128)} %collective-permute-done), kind=kLoop, calls=%fused_computation.17 | loop fusion | flops 5898240 | bytes 5898240 | tf_op jit(solution)/shard_map/div | solution.py:64
  86.4 0.8 fusion.16
  88.8 1.8 %fusion.124 = (f32[15,8,16,256]{3,2,1,0:T(8,128)S(1)}, f32[8,16,256]{2,1,0:T(8,128)S(1)}, f32[8,16,256]{2,1,0:T(8,128)S(1)}, f32[8,16,256]{2,1,0:T(8,128)S(1)}, ...) fusion(f32[15,8,16,256]{3,2,1,0:T(8,128)S(1)} %get-tuple-elemen, ...), kind=kLoop, calls=%fused_computation.217 | loop fusion | flops 5242880 | bytes 11665408
  91.8 1.0 fusion.33
  92.9 8.1 %collective-permute-start.5 = (f32[3,2,10,130]{3,2,1,0:T(8,128)S(1)}, f32[3,2,10,130]{3,2,1,0:T(8,128)S(1)}, u32[]{:S(2)}, u32[]{:S(2)}) collective-permute-start(f32[3,2,10,130]{3,2,1,0:T(8,128)S(1)} %slice.1039), channel_id=1, source_target_pairs={{1,0},{2,1},{3,2},{4,3},{5,4},{6,5},{7,6},{8,7},{9,8},{10,9},{11,1... | collective-permute-start | bytes 93608 | tf_op jit(solution)/shard_map/ppermute | solution.py:43
  103.3 0.7 copy-done.43
  104.1 0.6 copy.72
  106.0 5.9 %copy.76 = f32[3,24,16,128,2]{1,2,4,3,0:T(8,128)} copy(f32[3,24,16,128,2]{3,1,2,0,4:T(8,128)S(1)} %pad_maximum_fusion.3) | data formatting | bytes 2359296 | tf_op jit(solution)/shard_map/stack | solution.py:208
  111.9 6.6 %fusion.311 = (f32[1,22,16,256]{1,2,3,0:T(8,128)}, f32[1,22,16,256]{1,2,3,0:T(8,128)S(1)}, f32[1,22,16,256]{1,2,3,0:T(8,128)}) fusion(f32[3,24,16,256]{1,2,3,0:T(8,128)} %bitcast.1209), kind=kLoop, calls=%fused_computation.561 | loop fusion | bytes 2162688 | tf_op jit(solution)/shard_map/slice | solution.py:220
  118.5 1.9 %copy.82 = f32[1,22,16,256]{3,2,1,0:T(8,128)} copy(f32[1,22,16,256]{1,2,3,0:T(8,128)S(1)} %get-tuple-element.36) | data formatting | bytes 720896
  120.4 2.8 %copy.81 = f32[1,22,16,256]{3,2,1,0:T(8,128)S(1)} copy(f32[1,22,16,256]{1,2,3,0:T(8,128)} %get-tuple-element.37) | data formatting | bytes 720896
  123.2 2.6 %copy.83 = f32[1,22,16,256]{3,2,1,0:T(8,128)S(1)} copy(f32[1,22,16,256]{1,2,3,0:T(8,128)} %get-tuple-element.35) | data formatting | bytes 720896
  125.9 1.1 fusion.42
  127.6 0.6 add_multiply_fusion
  128.2 6.2 %divide_add_fusion = f32[5,17,16,256]{3,2,1,0:T(8,128)S(1)} fusion(f32[5,22,16,256]{3,2,1,0:T(8,128)S(1)} %get-tuple-element.39, f32[5,22,16,256]{3,2,1,0:T(8,128)S(1)} %get-tuple-element.38), kind=kLoop, calls=%fused_computation.43 | loop fusion | flops 44912640 | bytes 15319040 | tf_op jit(solution)/shard_map/add | solution.py:271
  134.5 1.2 fusion.19
  (144 shorter events, 8.1 us)
Async XLA Ops:
  0.6 4.1 %copy-start.2 = (f32[6,8,16,256]{3,2,1,0:T(8,128)S(1)}, f32[6,8,16,256]{3,2,1,0:T(8,128)}, u32[]{:S(2)}) copy-start(f32[6,8,16,256]{3,2,1,0:T(8,128)} %param.15) | copy-start | bytes 2359300
  0.6 4.1 %copy-start.9 = (f32[3,8,16,256]{3,2,1,0:T(8,128)S(1)}, f32[3,8,16,256]{3,2,1,0:T(8,128)}, u32[]{:S(2)}) copy-start(f32[3,8,16,256]{3,2,1,0:T(8,128)} %param.16) | copy-start | bytes 1179652
  4.8 9.3 %copy-start.6 = (f32[1,3,16,16,256]{4,3,2,1,0:T(8,128)S(1)}, f32[1,3,16,16,256]{4,3,2,1,0:T(8,128)}, u32[]{:S(2)}) copy-start(f32[1,3,16,16,256]{4,3,2,1,0:T(8,128)} %param.18) | copy-start | bytes 2359300
  4.8 9.2 %copy-start.7 = (f32[1,16,16,256]{3,2,1,0:T(8,128)S(1)}, f32[1,16,16,256]{3,2,1,0:T(8,128)}, u32[]{:S(2)}) copy-start(f32[1,16,16,256]{3,2,1,0:T(8,128)} %param.21) | copy-start | bytes 786436
  4.8 9.2 %copy-start.11 = (f32[1,3,16,16,256]{4,3,2,1,0:T(8,128)S(1)}, f32[1,3,16,16,256]{4,3,2,1,0:T(8,128)}, u32[]{:S(2)}) copy-start(f32[1,3,16,16,256]{4,3,2,1,0:T(8,128)} %param.20) | copy-start | bytes 2359300
  4.8 9.2 %copy-start.18 = (f32[1,16,16,256]{3,2,1,0:T(8,128)S(1)}, f32[1,16,16,256]{3,2,1,0:T(8,128)}, u32[]{:S(2)}) copy-start(f32[1,16,16,256]{3,2,1,0:T(8,128)} %param.19) | copy-start | bytes 786436
  4.8 9.2 %copy-start.19 = (f32[1,16,16,256]{3,2,1,0:T(8,128)S(1)}, f32[1,16,16,256]{3,2,1,0:T(8,128)}, u32[]{:S(2)}) copy-start(f32[1,16,16,256]{3,2,1,0:T(8,128)} %param.17) | copy-start | bytes 786436
  6.0 75.7 %collective-permute-start.1 = (f32[18,2,16,256]{3,2,1,0:T(8,128)}, f32[18,2,16,256]{3,2,1,0:T(8,128)}, u32[]{:S(2)}, u32[]{:S(2)}) collective-permute-start(f32[18,2,16,256]{3,2,1,0:T(8,128)} %get-tuple-element.41), channel_id=1, source_target_pairs={{1,0},{2,1},{3,2},{4,3},{5,4},{6,5},{7,6},{8,7},{9,8},{10,9},{11,1... | collective-permute-start | bytes 1769480 | tf_op jit(solution)/shard_map/ppermute | solution.py:23
  14.0 67.7 %collective-permute-start = (f32[18,2,16,256]{3,2,1,0:T(8,128)}, f32[18,2,16,256]{3,2,1,0:T(8,128)}, u32[]{:S(2)}, u32[]{:S(2)}) collective-permute-start(f32[18,2,16,256]{3,2,1,0:T(8,128)} %get-tuple-element.40), channel_id=1, source_target_pairs={{0,1},{1,2},{2,3},{3,4},{4,5},{5,6},{6,7},{7,8},{8,9},{9,10},{10,1... | collective-permute-start | bytes 1769480 | tf_op jit(solution)/shard_map/ppermute | solution.py:22
  40.9 37.8 %copy-start.39 = (f32[1,8,8,128]{3,2,1,0:T(8,128)}, f32[1,8,8,128]{3,2,1,0:T(8,128)S(1)}, u32[]{:S(2)}) copy-start(f32[1,8,8,128]{3,2,1,0:T(8,128)S(1)} %multiply_bitcast_fusion) | copy-start | bytes 98308
  41.5 46.4 %collective-permute-start.2 = (f32[1,1,8,128]{3,2,1,0:T(8,128)}, f32[1,1,8,128]{3,2,1,0:T(8,128)S(1)}, u32[]{:S(2)}, u32[]{:S(2)}) collective-permute-start(f32[1,1,8,128]{3,2,1,0:T(8,128)} %slice.1017), channel_id=1, source_target_pairs={{0,1},{1,2},{2,3},{3,4},{4,5},{5,6},{6,7},{7,8},{8,9},{9,10},{10,1... | collective-permute-start | bytes 12296 | tf_op jit(solution)/shard_map/ppermute | solution.py:37
  42.5 2.4 %copy-start.8 = (f32[1,16,16,256]{3,2,1,0:T(8,128)}, f32[1,16,16,256]{3,2,1,0:T(8,128)S(1)}, u32[]{:S(2)}) copy-start(f32[1,16,16,256]{3,2,1,0:T(8,128)S(1)} %slice_bitcast_fusion) | copy-start | bytes 786436
  44.9 33.9 %collective-permute-start.4 = (f32[7,3,16,256]{3,2,1,0:T(8,128)}, f32[7,3,16,256]{3,2,1,0:T(8,128)}, u32[]{:S(2)}, u32[]{:S(2)}) collective-permute-start(f32[7,3,16,256]{3,2,1,0:T(8,128)} %get-tuple-element.59), channel_id=1, source_target_pairs={{1,0},{2,1},{3,2},{4,3},{5,4},{6,5},{7,6},{8,7},{9,8},{10,9},{11,1... | collective-permute-start | bytes 1032200 | tf_op jit(solution)/shard_map/ppermute | solution.py:54
  52.7 26.0 %collective-permute-start.3 = (f32[7,3,16,256]{3,2,1,0:T(8,128)}, f32[7,3,16,256]{3,2,1,0:T(8,128)}, u32[]{:S(2)}, u32[]{:S(2)}) collective-permute-start(f32[7,3,16,256]{3,2,1,0:T(8,128)} %get-tuple-element.58), channel_id=1, source_target_pairs={{0,1},{1,2},{2,3},{3,4},{4,5},{5,6},{6,7},{7,8},{8,9},{9,10},{10,1... | collective-permute-start | bytes 1032200 | tf_op jit(solution)/shard_map/ppermute | solution.py:53
  64.1 3.0 %copy-start.10 = (f32[3,8,16,256]{3,2,1,0:T(8,128)S(1)}, f32[3,8,16,256]{3,2,1,0:T(8,128)}, u32[]{:S(2)}) copy-start(f32[3,8,16,256]{3,2,1,0:T(8,128)} %param.16) | copy-start | bytes 1179652
  64.1 3.8 %copy-start.1 = (f32[6,8,16,256]{3,2,1,0:T(8,128)S(1)}, f32[6,8,16,256]{3,2,1,0:T(8,128)}, u32[]{:S(2)}) copy-start(f32[6,8,16,256]{3,2,1,0:T(8,128)} %param.14) | copy-start | bytes 2359300
  67.2 1.6 %copy-start = (f32[8,16,256]{2,1,0:T(8,128)S(1)}, f32[8,16,256]{2,1,0:T(8,128)}, u32[]{:S(2)}) copy-start(f32[8,16,256]{2,1,0:T(8,128)} %param.11) | copy-start | bytes 393220
  68.8 2.7 %copy-start.20 = (f32[8,16,2]{2,1,0:T(8,128)}, f32[8,16,2]{2,1,0:T(8,128)S(1)}, u32[]{:S(2)}) copy-start(f32[8,16,2]{2,1,0:T(8,128)S(1)} %get-tuple-element.94) | copy-start | bytes 3076
  68.8 2.7 %copy-start.22 = (f32[8,16,2]{2,1,0:T(8,128)}, f32[8,16,2]{2,1,0:T(8,128)S(1)}, u32[]{:S(2)}) copy-start(f32[8,16,2]{2,1,0:T(8,128)S(1)} %get-tuple-element.95) | copy-start | bytes 3076
  68.9 2.6 %copy-start.12 = (f32[8,16,254]{2,1,0:T(8,128)}, f32[8,16,254]{2,1,0:T(8,128)S(1)}, u32[]{:S(2)}) copy-start(f32[8,16,254]{2,1,0:T(8,128)S(1)} %get-tuple-element.97) | copy-start | bytes 390148
  69.0 2.6 %copy-start.24 = (f32[8,16,1]{2,1,0:T(8,128)}, f32[8,16,1]{2,1,0:T(8,128)S(1)}, u32[]{:S(2)}) copy-start(f32[8,16,1]{2,1,0:T(8,128)S(1)} %get-tuple-element.98) | copy-start | bytes 1540
  69.0 2.6 %copy-start.26 = (f32[8,16,1]{2,1,0:T(8,128)}, f32[8,16,1]{2,1,0:T(8,128)S(1)}, u32[]{:S(2)}) copy-start(f32[8,16,1]{2,1,0:T(8,128)S(1)} %get-tuple-element.99) | copy-start | bytes 1540
  69.1 2.5 %copy-start.14 = (f32[8,16,255]{2,1,0:T(8,128)}, f32[8,16,255]{2,1,0:T(8,128)S(1)}, u32[]{:S(2)}) copy-start(f32[8,16,255]{2,1,0:T(8,128)S(1)} %get-tuple-element.100) | copy-start | bytes 391684
  69.2 2.5 %copy-start.16 = (f32[8,16,255]{2,1,0:T(8,128)}, f32[8,16,255]{2,1,0:T(8,128)S(1)}, u32[]{:S(2)}) copy-start(f32[8,16,255]{2,1,0:T(8,128)S(1)} %get-tuple-element.101) | copy-start | bytes 391684
  83.9 2.4 %copy-start.32 = (f32[8,16,256]{2,1,0:T(8,128)S(1)}, f32[8,16,256]{2,1,0:T(8,128)}, u32[]{:S(2)}) copy-start(f32[8,16,256]{2,1,0:T(8,128)} %get-tuple-element.67) | copy-start | bytes 393220
  83.9 2.4 %copy-start.33 = (f32[8,16,256]{2,1,0:T(8,128)S(1)}, f32[8,16,256]{2,1,0:T(8,128)}, u32[]{:S(2)}) copy-start(f32[8,16,256]{2,1,0:T(8,128)} %get-tuple-element.68) | copy-start | bytes 393220
  83.9 2.4 %copy-start.34 = (f32[8,16,256]{2,1,0:T(8,128)S(1)}, f32[8,16,256]{2,1,0:T(8,128)}, u32[]{:S(2)}) copy-start(f32[8,16,256]{2,1,0:T(8,128)} %get-tuple-element.69) | copy-start | bytes 393220
  87.3 1.0 copy-start.15
  87.3 1.0 copy-start.17
  87.3 1.0 copy-start.21
  87.3 1.0 copy-start.23
  87.4 1.1 copy-start.25
  87.4 1.1 copy-start.27
  87.4 1.2 copy-start.28
  87.4 1.2 copy-start.29
  87.4 1.2 copy-start.30
  87.4 1.3 copy-start.31
  87.4 1.3 copy-start.35
  87.4 1.3 copy-start.36
  87.4 1.4 copy-start.37
  87.5 1.4 %copy-start.38 = (f32[8,14,256]{2,1,0:T(8,128)S(1)}, f32[8,14,256]{2,1,0:T(8,128)}, u32[]{:S(2)}) copy-start(f32[8,14,256]{2,1,0:T(8,128)} %get-tuple-element.119) | copy-start | bytes 344068
  87.5 1.4 %slice-start = ((f32[1,8,8,128]{3,2,1,0:T(8,128)}), f32[1,7,8,128]{3,2,1,0:T(8,128)S(1)}, s32[]{:S(2)}) async-start(f32[1,8,8,128]{3,2,1,0:T(8,128)} %copy-done.39), calls=%async_computation | async-start | bytes 57344 | tf_op jit(solution)/shard_map/slice | solution.py:330
  87.5 1.4 %copy-start.40 = (f32[8,2,256]{2,1,0:T(2,128)S(1)}, f32[8,2,256]{2,1,0:T(2,128)}, u32[]{:S(2)}) copy-start(f32[8,2,256]{2,1,0:T(2,128)} %get-tuple-element.87) | copy-start | bytes 49156
  87.5 1.4 %copy-start.41 = (f32[8,2,256]{2,1,0:T(2,128)S(1)}, f32[8,2,256]{2,1,0:T(2,128)}, u32[]{:S(2)}) copy-start(f32[8,2,256]{2,1,0:T(2,128)} %get-tuple-element.116) | copy-start | bytes 49156
  87.5 1.4 copy-start.42
  92.9 10.2 %collective-permute-start.5 = (f32[3,2,10,130]{3,2,1,0:T(8,128)S(1)}, f32[3,2,10,130]{3,2,1,0:T(8,128)S(1)}, u32[]{:S(2)}, u32[]{:S(2)}) collective-permute-start(f32[3,2,10,130]{3,2,1,0:T(8,128)S(1)} %slice.1039), channel_id=1, source_target_pairs={{1,0},{2,1},{3,2},{4,3},{5,4},{6,5},{7,6},{8,7},{9,8},{10,9},{11,1... | collective-permute-start | bytes 93608 | tf_op jit(solution)/shard_map/ppermute | solution.py:43
  102.8 1.3 copy-start.43
  120.4 5.4 %copy-start.3 = (f32[7,22,16,256]{3,2,1,0:T(8,128)S(1)}, f32[7,22,16,256]{3,2,1,0:T(8,128)}, u32[]{:S(2)}) copy-start(f32[7,22,16,256]{3,2,1,0:T(8,128)} %pad_maximum_fusion) | copy-start | bytes 7569412
  (3 other events, 2.8 us)
where the time goes:
time: 137 us; the launch traced here: 136 us
  local copies, waits for them, and re-layouts  64.4 us (47%)
  other arithmetic  43.7 us (32%)
  starting transfers between devices  26.1 us (19%)
  between operations  1.52 us (1%)
    reshape x1, local copies, waits for them, and re-layouts, restrict(): fine_cells.reshape(leading + (extent_x // 2, 2, extent_y // 2, 2, extent_...  18.8 us
    unnamed x96, local copies, waits for them, and re-layouts  13.3 us
    ppermute x1, starting transfers between devices, from_behind(): return lax.ppermute(array, axis, pairs)  8.08 us
    ppermute x1, starting transfers between devices, extended(): lax.ppermute(leading, axis, [(b, a) for a, b in up])  8.01 us
    ppermute x1, starting transfers between devices, extended_2(): after = lax.ppermute(leading, axis, down)  7.86 us
    div x3, other arithmetic, rfirst(): (jnp.roll(values, 2, direction) - 8.0 * jnp.roll(values, 1, direction) +...  7.47 us
    reduce_sum x1, other arithmetic, restrict(): return jnp.sum(blocks, axis=(-5, -3, -1)) * 0.125  6.98 us
    slice x8, local copies, waits for them, and re-layouts, rfirst(): jnp.roll(values, -1, direction)  6.72 us
  transfers between devices with their start and end apart: 6, of which 0 were waited for; matrix products, arithmetic and copies ran while one was open for 48% of the time, Pallas kernels for 0%

commit v1 on v0

v1 whole, which is shorter than its diff:
```python
import functools
import math

import jax
import jax.numpy as jnp
from jax import lax
from jax.experimental import pallas as pl
from jax.experimental.pallas import tpu as pltpu
from jax.sharding import PartitionSpec as P

MESH = pl.DeviceIdType.MESH
F32 = jnp.float32
EXACT = lax.Precision.HIGHEST

pair_index = ((0, 1, 2), (1, 3, 4), (2, 4, 5))
sym_pairs = ((0, 0), (0, 1), (0, 2), (1, 1), (1, 2), (2, 2))

LAPSE, CONF, CURV, METRIC, TRACE, SHIFT = 0, 1, 2, 3, 9, 15
COARSE, FINE = 8, 16
CY, CZ = 16, 256
LANES = 128


def total(terms):
    return functools.reduce(lambda x, y: x + y, terms)


def ring_first(v, axis):
    n = v.shape[axis]
    far = pltpu.roll(v, 2, axis) - pltpu.roll(v, n - 2, axis)
    near = pltpu.roll(v, n - 1, axis) - pltpu.roll(v, 1, axis)
    return far + 8.0 * near


def ring_second(v, axis):
    n = v.shape[axis]
    far = pltpu.roll(v, 2, axis) + pltpu.roll(v, n - 2, axis)
    near = pltpu.roll(v, n - 1, axis) + pltpu.roll(v, 1, axis)
    return 16.0 * near - far - 30.0 * v


def x_first(mp, f, r):
    return (mp[f, r - 2] - mp[f, r + 2]) + 8.0 * (mp[f, r + 1] - mp[f, r - 1])


def derivatives(mp, ob, dd, i):
    r = i + 2
    by12 = mp[SHIFT + 1, r] * (1.0 / 12.0)
    bz12 = mp[SHIFT + 2, r] * (1.0 / 12.0)
    for f in range(2, SHIFT):
        v = mp[f, r]
        ob[f, i] = by12 * ring_first(v, 0) + bz12 * ring_first(v, 1)
    bx12 = mp[SHIFT, r] * (1.0 / 12.0)
    for f in (LAPSE, CONF):
        v = mp[f, r]
        along = x_first(mp, f, r)
        ob[f, i] = bx12 * along + by12 * ring_first(v, 0) + bz12 * ring_first(v, 1)
        if f == LAPSE:
            dd[10] = ring_first(along, 0) * (1.0 / 144.0)
            dd[11] = ring_first(along, 1) * (1.0 / 144.0)
    v = mp[LAPSE, r]
    dd[9] = (16.0 * (mp[LAPSE, r - 1] + mp[LAPSE, r + 1]) - (mp[LAPSE, r - 2] + mp[LAPSE, r + 2]) - 30.0 * v) * (1.0 / 12.0)
    dd[12] = ring_second(v, 0) * (1.0 / 12.0)
    dd[13] = ring_first(ring_first(v, 1), 0) * (1.0 / 144.0)
    dd[14] = ring_second(v, 1) * (1.0 / 12.0)
    for k in range(3):
        v = mp[SHIFT + k, r]
        dd[k] = x_first(mp, SHIFT + k, r) * (1.0 / 12.0)
        dd[3 + k] = ring_first(v, 0) * (1.0 / 12.0)
        dd[6 + k] = ring_first(v, 1) * (1.0 / 12.0)


def rates(mp, ob, dd, i, tile):
    r = i + 2
    al, ch, kk = [mp[(f, r) + tile] for f in (LAPSE, CONF, CURV)]
    g = [mp[(METRIC + p, r) + tile] for p in range(6)]
    ds = [[dd[(3 * k + j,) + tile] for j in range(3)] for k in range(3)]
    hess = [dd[(9 + p,) + tile] for p in range(6)]
    div = ds[0][0] + ds[1][1] + ds[2][2]
    tdiv = div * (2.0 / 3.0)
    a, b, c, d, e, f = g
    cof = (d * f - e * e, c * e - b * f, b * e - c * d, a * f - c * c, b * c - a * e, a * d - b * b)
    rdet = 1.0 / (a * cof[0] + b * cof[1] + c * cof[2])
    inv = [entry * rdet for entry in cof]
    alk = al * kk
    al2 = 2.0 * al
    ob[(0, i) + tile] = ob[(0, i) + tile] - 2.0 * alk
    ob[(1, i) + tile] = ob[(1, i) + tile] + (2.0 / 3.0) * ch * (alk - div)
    trh = (inv[0] * hess[0] + inv[3] * hess[3] + inv[5] * hess[5]) + 2.0 * (inv[1] * hess[1] + inv[2] * hess[2] + inv[4] * hess[4])
    cv = [mp[(TRACE + p, r) + tile] for p in range(6)]
    mixed = [[total([cv[pair_index[p][k]] * inv[pair_index[k][q]] for k in range(3)]) for q in range(3)] for p in range(3)]
    square = (mixed[0][0] * mixed[0][0] + mixed[1][1] * mixed[1][1] + mixed[2][2] * mixed[2][2]) + 2.0 * (
        mixed[0][1] * mixed[1][0] + mixed[0][2] * mixed[2][0] + mixed[1][2] * mixed[2][1]
    )
    chtr = ch * trh
    ob[(2, i) + tile] = ob[(2, i) + tile] - chtr + al * (square + kk * kk * (1.0 / 3.0))
    chtr3 = chtr * (1.0 / 3.0)
    scale = alk - tdiv
    for p, (x, y) in enumerate(sym_pairs):
        if x == y:
            moved_g = 2.0 * total([g[pair_index[x][k]] * ds[x][k] for k in range(3)])
            moved_c = 2.0 * total([cv[pair_index[x][k]] * ds[x][k] for k in range(3)])
        else:
            moved_g = total([g[pair_index[x][k]] * ds[y][k] + g[pair_index[y][k]] * ds[x][k] for k in range(3)])
            moved_c = total([cv[pair_index[x][k]] * ds[y][k] + cv[pair_index[y][k]] * ds[x][k] for k in range(3)])
        ob[(3 + p, i) + tile] = ob[(3 + p, i) + tile] - al2 * cv[p] + moved_g - tdiv * g[p]
        product = total([mixed[x][k] * cv[pair_index[k][y]] for k in range(3)])
        ob[(9 + p, i) + tile] = ob[(9 + p, i) + tile] + scale * cv[p] - al2 * product + moved_c - ch * hess[p] + chtr3 * g[p]


def advect_x(mp, ob, src, i):
    r = i + 2
    bx12 = mp[SHIFT, r] * (1.0 / 12.0)
    for f in range(2, SHIFT):
        moved = bx12 * x_first(mp, f, r)
        if f == CURV:
            moved = moved + (4.0 * math.pi) * mp[LAPSE, r] * src[i]
        ob[f, i] = ob[f, i] + moved


def split_flux(fl, fine, fpm, jj, keep):
    odd = jj % 2
    t = (jj + 1) // 2
    u = t + 1 - 2 * odd
    lapse, shift, conf = [0.75 * fine[m, t] + 0.25 * fine[m, u] for m in range(3)]
    vel, pres = fl[5, jj], fl[6, jj]
    root = lax.rsqrt(conf)
    weight = lapse * (root * root * root) * pres
    moved = lapse * vel - shift
    speed = lapse + jnp.abs(shift)
    plus = 0.5 * (moved + speed)
    minus = 0.5 * (moved - speed)
    half = 0.5 * weight
    extra = (None, half, None, None, half * vel)
    for n in range(5):
        v = fl[n, jj]
        fp, fm = v * plus, v * minus
        if extra[n] is not None:
            fp, fm = fp + extra[n], fm + extra[n]
        if keep is not None:
            fp, fm = jnp.where(keep, fp, 0.0), jnp.where(keep, fm, 0.0)
        fpm[n, jj] = fp
        fpm[5 + n, jj] = fm


def cell_terms(v):
    e = [v[k + 1] - v[k] for k in range(len(v) - 1)]
    h, s0, s1, s2 = [None], [None], [None], [None]
    for k in range(1, len(v) - 1):
        hk = 0.5 * (e[k] - e[k - 1])
        ck = (13.0 / 3.0) * (hk * hk) + 1e-6
        tp, tm, mid = hk + e[k], hk - e[k - 1], e[k] - hk
        h.append(hk)
        s0.append(ck + tp * tp)
        s1.append(ck + mid * mid)
        s2.append(ck + tm * tm)
    return h, s0, s1, s2


def correction(s0, s1, s2, h0, h1, h2):
    p12, p02, p01 = s1 * s2, s0 * s2, s0 * s1
    w0, w1, w2 = p12 * p12, 6.0 * (p02 * p02), 3.0 * (p01 * p01)
    top = w0 * (2.0 * h0 - 3.0 * h1) - w1 * h1 - w2 * h2
    return top / (3.0 * (w0 + w1 + w2))


def weno(fpm, oh, first, faces, n, tile):
    layers = faces + 5
    fp = [fpm[(n, first + k) + tile] for k in range(layers)]
    fm = [fpm[(5 + n, first + k) + tile] for k in range(layers)]
    hp, p0, p1, p2 = cell_terms(fp)
    hm, m0, m1, m2 = cell_terms(fm)
    flux = [fp[k] + fm[k] for k in range(2, layers - 2)]
    last = None
    for q in range(faces):
        k = q + 2
        face = 0.5 * (flux[q] + flux[q + 1])
        face = face + correction(p0[k - 1], p1[k], p2[k + 1], hp[k - 1], hp[k], hp[k + 1])
        face = face + correction(m2[k + 2], m1[k + 1], m0[k], hm[k + 2], hm[k + 1], hm[k])
        if last is not None:
            oh[(n, first + k - 3) + tile] = 2.0 * (last - face)
        last = face


def iota2(shape, dim):
    return lax.broadcasted_iota(jnp.int32, shape, dim)


def refine_weights(fine_pos, coarse_pos, start):
    center = start + fine_pos // 2
    side = center + 2 * (fine_pos % 2) - 1
    return jnp.where(coarse_pos == center, 0.75, jnp.where(coarse_pos == side, 0.25, 0.0)).astype(F32)


def make_fine(mp, fine, py, pz):
    for m, f in enumerate((LAPSE, SHIFT, CONF)):
        for part in range(2):
            coarse = mp[f, 1 + 6 * part : 7 + 6 * part].reshape(6 * CY, CZ)
            wide = jnp.dot(py[...], coarse, precision=EXACT, preferred_element_type=F32)
            wide = jnp.dot(wide, pz[...], precision=EXACT, preferred_element_type=F32)
            fine[m, 6 * part : 6 * part + 6] = wide.reshape(6, CY, CZ)


def make_sources(fl, vyz, summed, src, plane, ry, rz):
    def pair(c, _):
        cells = []
        for s in range(2):
            j = 2 * c + s
            q = j + 3
            dot = fl[1, q] * fl[5, q] + fl[2, q] * vyz[0, j] + fl[3, q] * vyz[1, j]
            cells.append(fl[4, q] + fl[0, q] + dot + 3.0 * fl[6, q])
        summed[c] = cells[0] + cells[1]
        return 0

    lax.fori_loop(0, COARSE, pair, 0)
    level = jnp.dot(summed[...].reshape(COARSE * CY, CZ), rz[...], precision=EXACT, preferred_element_type=F32)
    level = jnp.dot(ry[...], level, precision=EXACT, preferred_element_type=F32).reshape(COARSE, CY, CZ)
    src[1:COARSE] = level[: COARSE - 1]
    plane[...] = level[COARSE - 1]


def kernel(sizes, lapse, conf, curv, metric, trace, shift, dens, mom, ener, vel, pres, ob, oh,
           mp, fl, vyz, src, plane, summed, dd, fine, fpm, py, pz, ry, rz, lsem, ssem, rsem):
    stars, blocks = sizes
    count = stars * blocks
    blk = lax.axis_index("blk")
    me = lax.axis_index("star") * blocks + blk
    up = lax.rem(me + 1, count)
    down = lax.rem(me + count - 1, count)
    up = (up // blocks, lax.rem(up, blocks))
    down = (down // blocks, lax.rem(down, blocks))

    barrier = pltpu.get_barrier_semaphore()
    for device in (up, down):
        pl.semaphore_signal(barrier, inc=1, device_id=device, device_id_type=MESH)

    own = pl.ds(2, COARSE)
    fown = pl.ds(3, FINE)
    loads = [
        pltpu.make_async_copy(source, target, lsem.at[k])
        for k, (source, target) in enumerate((
            (dens.at[0], fl.at[0, fown]),
            (mom.at[0], fl.at[pl.ds(1, 3), fown]),
            (ener.at[0], fl.at[4, fown]),
            (vel.at[0, 0], fl.at[5, fown]),
            (pres.at[0], fl.at[6, fown]),
            (vel.at[0, pl.ds(1, 2)], vyz),
            (shift, mp.at[pl.ds(SHIFT, 3), own]),
            (lapse, mp.at[LAPSE, own]),
            (conf, mp.at[CONF, own]),
            (curv, mp.at[CURV, own]),
            (metric, mp.at[pl.ds(METRIC, 6), own]),
            (trace, mp.at[pl.ds(TRACE, 6), own]),
        ))
    ]
    for copy in loads:
        copy.start()
    pl.semaphore_wait(barrier, 2)

    sends = []

    def send(source, target, device):
        k = len(sends)
        copy = pltpu.make_async_remote_copy(
            src_ref=source, dst_ref=target, send_sem=ssem.at[k], recv_sem=rsem.at[k], device_id=device, device_id_type=MESH
        )
        copy.start()
        sends.append(copy)
        return copy

    top, bottom = pl.ds(COARSE - 2, 2), pl.ds(0, 2)
    low, high = pl.ds(0, 2), pl.ds(COARSE + 2, 2)
    high3 = pl.ds(COARSE + 2, 3)
    ftop, flow, fhigh = pl.ds(FINE - 3, 3), pl.ds(0, 3), pl.ds(FINE + 3, 3)
    first = [
        send(shift.at[:, top], mp.at[pl.ds(SHIFT, 3), low], up),
        send(shift.at[0, flow], mp.at[SHIFT, high3], down),
        send(shift.at[pl.ds(1, 2), bottom], mp.at[pl.ds(SHIFT + 1, 2), high], down),
        send(lapse.at[top], mp.at[LAPSE, low], up),
        send(lapse.at[flow], mp.at[LAPSE, high3], down),
        send(conf.at[top], mp.at[CONF, low], up),
        send(conf.at[flow], mp.at[CONF, high3], down),
    ]
    second = []
    for source, target in (
        (lambda s: dens.at[0, s], lambda s: fl.at[0, s]),
        (lambda s: mom.at[0, :, s], lambda s: fl.at[pl.ds(1, 3), s]),
        (lambda s: ener.at[0, s], lambda s: fl.at[4, s]),
        (lambda s: vel.at[0, 0, s], lambda s: fl.at[5, s]),
        (lambda s: pres.at[0, s], lambda s: fl.at[6, s]),
    ):
        second.append(send(source(ftop), target(flow), up))
        second.append(send(source(flow), target(fhigh), down))
    third = [
        send(curv.at[top], mp.at[CURV, low], up),
        send(curv.at[bottom], mp.at[CURV, high], down),
        send(metric.at[:, top], mp.at[pl.ds(METRIC, 6), low], up),
        send(metric.at[:, bottom], mp.at[pl.ds(METRIC, 6), high], down),
        send(trace.at[:, top], mp.at[pl.ds(TRACE, 6), low], up),
        send(trace.at[:, bottom], mp.at[pl.ds(TRACE, 6), high], down),
    ]

    def same_block(shape):
        return iota2(shape, 0) // CY == iota2(shape, 1) // CY

    shape = (6 * CY, 6 * CY)
    py[...] = jnp.where(same_block(shape), refine_weights(iota2(shape, 0) % CY, iota2(shape, 1) % CY, CY // 4), 0.0)
    shape = (CZ, CZ)
    pz[...] = refine_weights(iota2(shape, 1), iota2(shape, 0), CZ // 4)
    rz[...] = jnp.where(CZ // 4 + iota2(shape, 0) // 2 == iota2(shape, 1), 0.125, 0.0).astype(F32)
    shape = (COARSE * CY, COARSE * CY)
    ry[...] = jnp.where(
        same_block(shape) & (CY // 4 + iota2(shape, 1) % CY // 2 == iota2(shape, 0) % CY), 1.0, 0.0
    ).astype(F32)

    for copy in loads[:6]:
        copy.wait()
    make_sources(fl, vyz, summed, src, plane, ry, rz)
    third.append(send(plane, src.at[0], up))
    for copy in loads[6:]:
        copy.wait()

    tiles = [(pl.ds(8 * y, 8), pl.ds(LANES * z, LANES)) for y in range(CY // 8) for z in range(CZ // LANES)]

    def tile_at(t):
        return (pl.ds(pl.multiple_of(t // 2 * 8, 8), 8), pl.ds(pl.multiple_of(t % 2 * LANES, LANES), LANES))

    def metric_layer(i):
        derivatives(mp, ob, dd, i)

        def one(t, _):
            rates(mp, ob, dd, i, tile_at(t))
            return 0

        lax.fori_loop(0, len(tiles), one, 0)

    def inner(i, _):
        metric_layer(i)
        advect_x(mp, ob, src, i)
        return 0

    def edge(k):
        return k + k // 2 * (COARSE - 4)

    def outer(k, _):
        metric_layer(edge(k))
        return 0

    def last(k, _):
        advect_x(mp, ob, src, edge(k))
        return 0

    lax.fori_loop(2, COARSE - 2, inner, 0)
    for copy in first:
        copy.wait_recv()
    lax.fori_loop(0, 4, outer, 0)
    make_fine(mp, fine, py, pz)

    def flux_own(jj, _):
        split_flux(fl, fine, fpm, jj, None)
        return 0

    lax.fori_loop(3, FINE + 3, flux_own, 0)

    def weno_inner(q, _):
        weno(fpm, oh, 3, FINE - 5, q // 4, tile_at(q % 4))
        return 0

    lax.fori_loop(0, 20, weno_inner, 0)

    for copy in second:
        copy.wait_recv()
    for jj in range(3):
        split_flux(fl, fine, fpm, jj, blk != 0)
        split_flux(fl, fine, fpm, FINE + 3 + jj, blk != blocks - 1)

    def weno_outer(q, _):
        weno(fpm, oh, 0, 4, q // 4, tile_at(q % 4))
        weno(fpm, oh, FINE - 3, 4, q // 4, tile_at(q % 4))
        return 0

    lax.fori_loop(0, 20, weno_outer, 0)

    for copy in third:
        copy.wait_recv()
    lax.fori_loop(0, 4, last, 0)
    for copy in sends:
        copy.wait_send()


def write_out(pb, ph, ob, oh, sem):
    copies = [pltpu.make_async_copy(pb, ob, sem.at[0]), pltpu.make_async_copy(ph, oh.at[0], sem.at[1])]
    for copy in copies:
        copy.start()
    for copy in copies:
        copy.wait()


def on_device(sizes, *arrays):
    hbm = pl.BlockSpec(memory_space=pltpu.HBM)
    vmem = pl.BlockSpec(memory_space=pltpu.VMEM)
    metric_out, fluid_out = (15, COARSE, CY, CZ), (5, FINE, CY, CZ)
    part = pl.pallas_call(
        functools.partial(kernel, sizes),
        out_shape=(pltpu.VMEM(metric_out, F32), pltpu.VMEM(fluid_out, F32)),
        in_specs=[hbm] * 11,
        out_specs=(vmem, vmem),
        scratch_shapes=[
            pltpu.VMEM((18, COARSE + 5, CY, CZ), F32),
            pltpu.VMEM((7, FINE + 6, CY, CZ), F32),
            pltpu.VMEM((2, FINE, CY, CZ), F32),
            pltpu.VMEM((COARSE, CY, CZ), F32),
            pltpu.VMEM((CY, CZ), F32),
            pltpu.VMEM((COARSE, CY, CZ), F32),
            pltpu.VMEM((15, CY, CZ), F32),
            pltpu.VMEM((3, 12, CY, CZ), F32),
            pltpu.VMEM((10, FINE + 6, CY, CZ), F32),
            pltpu.VMEM((6 * CY, 6 * CY), F32),
            pltpu.VMEM((CZ, CZ), F32),
            pltpu.VMEM((COARSE * CY, COARSE * CY), F32),
            pltpu.VMEM((CZ, CZ), F32),
            pltpu.SemaphoreType.DMA((12,)),
            pltpu.SemaphoreType.DMA((24,)),
            pltpu.SemaphoreType.DMA((24,)),
        ],
        compiler_params=pltpu.CompilerParams(collective_id=0, has_side_effects=True, vmem_limit_bytes=58 << 20),
        cost_estimate=pl.CostEstimate(flops=60_000_000, bytes_accessed=8_000_000, transcendentals=0),
    )(*arrays)
    anywhere = pl.BlockSpec(memory_space=pl.ANY)
    return pl.pallas_call(
        write_out,
        out_shape=(jax.ShapeDtypeStruct(metric_out, F32), jax.ShapeDtypeStruct((1,) + fluid_out, F32)),
        in_specs=[vmem] * 2,
        out_specs=(anywhere, anywhere),
        scratch_shapes=[pltpu.SemaphoreType.DMA((2,))],
        compiler_params=pltpu.CompilerParams(vmem_limit_bytes=16 << 20),
        cost_estimate=pl.CostEstimate(flops=0, bytes_accessed=6_400_000, transcendentals=0),
    )(*part)


def solution(mesh):
    level = P(("star", "blk"), None, None)
    level4 = P(None, ("star", "blk"), None, None)
    box = P("star", "blk", None, None)
    box5 = P("star", None, "blk", None, None)
    sizes = (mesh.shape["star"], mesh.shape["blk"])
    return jax.shard_map(
        functools.partial(on_device, sizes),
        mesh=mesh,
        in_specs=(level, level, level, level4, level4, level4, box, box5, box, box5, box),
        out_specs=(level4, box5),
        check_vma=False,
    )
```

time: 137 us -> 26.1 us (0.19)
  the two profiles are of different devices: /device:TPU:6 before, /device:TPU:1 now
where the time goes in v1:
time: 26.1 us; the launch traced here: 26 us
  Pallas kernels  25.3 us (97%)
  between operations  0.64 us (2%)
    pallas_call x1, Pallas kernels, on_device(): pl.pallas_call(functools.partial(kernel, sizes), out_shape=(pltpu.VMEM(me...  23.6 us
    pallas_call x1, Pallas kernels, on_device(): pl.pallas_call(write_out, out_shape=(jax.ShapeDtypeStruct(metric_out, F32...  1.72 us

profile of v1, /device:TPU:1, one launch (start us, length us, event | category | flops | bytes accessed | tf_op | source)
XLA Modules:
  0.0 26.0 jit_solution(1913551692642555744)
XLA Ops:
  0.6 23.6 %shard_map.122 = (f32[15,8,16,256]{3,2,1,0:T(8,128)S(1)}, f32[5,16,16,256]{3,2,1,0:T(8,128)S(1)}) custom-call(f32[8,16,256]{2,1,0:T(8,128)} %lapse.1, f32[8,16,256]{2,1,0:T(8,128)} %conf.1, f32[8,16,256]{2,1,0:T(8,128)} %curv.1, f32[6,8,16,256]{3,2,1,0:T(8,128)} %metric.1, f32[6,8,16,256]{3,2,1,0:T(8,128)} %trace.1, f32[3,8,16,256]{3,2,1,0:T(8,128)} %shift.1, ...), custom_call_target="tpu_custom_call" | custom-call | flops 60000000 | bytes 8000000 | tf_op jit(solution)/shard_map/pallas_call | solution.py:403
  24.3 1.7 %shard_map.123 = (f32[15,8,16,256]{3,2,1,0:T(8,128)}, f32[1,5,16,16,256]{4,3,2,1,0:T(8,128)}) custom-call(f32[15,8,16,256]{3,2,1,0:T(8,128)S(1)} %get-tuple-element.4.pb, f32[5,16,16,256]{3,2,1,0:T(8,128)S(1)} %get-tuple-element.5.ph), custom_call_target="tpu_custom_call" | custom-call | bytes 6400000 | tf_op jit(solution)/shard_map/pallas_call | solution.py:430

commit v2 on v1

--- a/solution.py
+++ b/solution.py
@@ -10,7 +10,6 @@
 
 MESH = pl.DeviceIdType.MESH
 F32 = jnp.float32
-EXACT = lax.Precision.HIGHEST
 
 pair_index = ((0, 1, 2), (1, 3, 4), (2, 4, 5))
 sym_pairs = ((0, 0), (0, 1), (0, 2), (1, 1), (1, 2), (2, 2))
@@ -25,18 +24,34 @@
     return functools.reduce(lambda x, y: x + y, terms)
 
 
+def rolled(v, axis):
+    n = v.shape[axis]
+    if axis == 1:
+        return [pltpu.roll(v, s, 1) for s in (2, 1, n - 1, n - 2)]
+    low, high = v[:8], v[8:]
+    row = iota2(low.shape, 0)
+    out = []
+    for s in (2, 1, 7, 6):
+        a, b = pltpu.roll(low, s, 0), pltpu.roll(high, s, 0)
+        wrapped = row < s
+        if s < 4:
+            parts = [jnp.where(wrapped, b, a), jnp.where(wrapped, a, b)]
+        else:
+            parts = [jnp.where(wrapped, a, b), jnp.where(wrapped, b, a)]
+        out.append(jnp.concatenate(parts, 0))
+    return out
+
+
+def first_of(moved):
+    return (moved[0] - moved[3]) + 8.0 * (moved[2] - moved[1])
+
+
+def second_of(v, moved):
+    return 16.0 * (moved[1] + moved[2]) - (moved[0] + moved[3]) - 30.0 * v
+
+
 def ring_first(v, axis):
-    n = v.shape[axis]
-    far = pltpu.roll(v, 2, axis) - pltpu.roll(v, n - 2, axis)
-    near = pltpu.roll(v, n - 1, axis) - pltpu.roll(v, 1, axis)
-    return far + 8.0 * near
-
-
-def ring_second(v, axis):
-    n = v.shape[axis]
-    far = pltpu.roll(v, 2, axis) + pltpu.roll(v, n - 2, axis)
-    near = pltpu.roll(v, n - 1, axis) + pltpu.roll(v, 1, axis)
-    return 16.0 * near - far - 30.0 * v
+    return first_of(rolled(v, axis))
 
 
 def x_first(mp, f, r):
@@ -54,15 +69,17 @@
     for f in (LAPSE, CONF):
         v = mp[f, r]
         along = x_first(mp, f, r)
-        ob[f, i] = bx12 * along + by12 * ring_first(v, 0) + bz12 * ring_first(v, 1)
+        ys, zs = rolled(v, 0), rolled(v, 1)
+        dz = first_of(zs)
+        ob[f, i] = bx12 * along + by12 * first_of(ys) + bz12 * dz
         if f == LAPSE:
             dd[10] = ring_first(along, 0) * (1.0 / 144.0)
             dd[11] = ring_first(along, 1) * (1.0 / 144.0)
+            dd[12] = second_of(v, ys) * (1.0 / 12.0)
+            dd[13] = ring_first(dz, 0) * (1.0 / 144.0)
+            dd[14] = second_of(v, zs) * (1.0 / 12.0)
     v = mp[LAPSE, r]
     dd[9] = (16.0 * (mp[LAPSE, r - 1] + mp[LAPSE, r + 1]) - (mp[LAPSE, r - 2] + mp[LAPSE, r + 2]) - 30.0 * v) * (1.0 / 12.0)
-    dd[12] = ring_second(v, 0) * (1.0 / 12.0)
-    dd[13] = ring_first(ring_first(v, 1), 0) * (1.0 / 144.0)
-    dd[14] = ring_second(v, 1) * (1.0 / 12.0)
     for k in range(3):
         v = mp[SHIFT + k, r]
         dd[k] = x_first(mp, SHIFT + k, r) * (1.0 / 12.0)
@@ -145,40 +162,42 @@
 
 def cell_terms(v):
     e = [v[k + 1] - v[k] for k in range(len(v) - 1)]
-    h, s0, s1, s2 = [None], [None], [None], [None]
+    d, z0, z1, z2 = [None], [None], [None], [None]
     for k in range(1, len(v) - 1):
-        hk = 0.5 * (e[k] - e[k - 1])
-        ck = (13.0 / 3.0) * (hk * hk) + 1e-6
-        tp, tm, mid = hk + e[k], hk - e[k - 1], e[k] - hk
-        h.append(hk)
-        s0.append(ck + tp * tp)
-        s1.append(ck + mid * mid)
-        s2.append(ck + tm * tm)
-    return h, s0, s1, s2
-
-
-def correction(s0, s1, s2, h0, h1, h2):
-    p12, p02, p01 = s1 * s2, s0 * s2, s0 * s1
-    w0, w1, w2 = p12 * p12, 6.0 * (p02 * p02), 3.0 * (p01 * p01)
-    top = w0 * (2.0 * h0 - 3.0 * h1) - w1 * h1 - w2 * h2
-    return top / (3.0 * (w0 + w1 + w2))
-
-
-def weno(fpm, oh, first, faces, n, tile):
-    layers = faces + 5
-    fp = [fpm[(n, first + k) + tile] for k in range(layers)]
-    fm = [fpm[(5 + n, first + k) + tile] for k in range(layers)]
-    hp, p0, p1, p2 = cell_terms(fp)
-    hm, m0, m1, m2 = cell_terms(fm)
-    flux = [fp[k] + fm[k] for k in range(2, layers - 2)]
+        dk = e[k] - e[k - 1]
+        mid = e[k] + e[k - 1]
+        square = dk * dk
+        flat = mid * mid + 4e-6
+        s1 = flat + (13.0 / 3.0) * square
+        both = flat + (25.0 / 3.0) * square
+        cross = (4.0 * dk) * mid
+        s0, s2 = both + cross, both - cross
+        d.append(dk)
+        z0.append(s0 * s0)
+        z1.append(s1 * s1)
+        z2.append(s2 * s2)
+    return d, z0, z1, z2
+
+
+def correction(z0, z1, z2, d0, d1, d2):
+    w0, w1, w2 = 1.0 / z0, 2.0 / z1, 1.0 / z2
+    top = w0 * ((2.0 / 3.0) * d0 - d1) - (w1 * d1 + w2 * d2)
+    return top * (1.0 / (w0 + 3.0 * (w1 + w2)))
+
+
+def weno(fpm, oh, n, tile):
+    layers = FINE + 6
+    fp = [fpm[(n, k) + tile] for k in range(layers)]
+    fm = [fpm[(5 + n, k) + tile] for k in range(layers)]
+    dp, p0, p1, p2 = cell_terms(fp)
+    dm, m0, m1, m2 = cell_terms(fm)
     last = None
-    for q in range(faces):
-        k = q + 2
-        face = 0.5 * (flux[q] + flux[q + 1])
-        face = face + correction(p0[k - 1], p1[k], p2[k + 1], hp[k - 1], hp[k], hp[k + 1])
-        face = face + correction(m2[k + 2], m1[k + 1], m0[k], hm[k + 2], hm[k + 1], hm[k])
+    for k in range(2, layers - 3):
+        face = (fp[k] + fm[k]) + (fp[k + 1] + fm[k + 1])
+        face = face + correction(p0[k - 1], p1[k], p2[k + 1], dp[k - 1], dp[k], dp[k + 1])
+        face = face + correction(m2[k + 2], m1[k + 1], m0[k], dm[k + 2], dm[k + 1], dm[k])
         if last is not None:
-            oh[(n, first + k - 3) + tile] = 2.0 * (last - face)
+            oh[(n, k - 3) + tile] = last - face
         last = face
 
 
@@ -192,13 +211,28 @@
     return jnp.where(coarse_pos == center, 0.75, jnp.where(coarse_pos == side, 0.25, 0.0)).astype(F32)
 
 
+def thirds(v):
+    high = v.astype(jnp.bfloat16)
+    rest = v - high.astype(F32)
+    mid = rest.astype(jnp.bfloat16)
+    low = (rest - mid.astype(F32)).astype(jnp.bfloat16)
+    return [high, mid, low]
+
+
+def times(v, weights):
+    return jnp.dot(jnp.concatenate(thirds(v), 1), weights, preferred_element_type=F32)
+
+
+def applied(weights, v):
+    return jnp.dot(weights, jnp.concatenate(thirds(v), 0), preferred_element_type=F32)
+
+
 def make_fine(mp, fine, py, pz):
     for m, f in enumerate((LAPSE, SHIFT, CONF)):
-        for part in range(2):
-            coarse = mp[f, 1 + 6 * part : 7 + 6 * part].reshape(6 * CY, CZ)
-            wide = jnp.dot(py[...], coarse, precision=EXACT, preferred_element_type=F32)
-            wide = jnp.dot(wide, pz[...], precision=EXACT, preferred_element_type=F32)
-            fine[m, 6 * part : 6 * part + 6] = wide.reshape(6, CY, CZ)
+        wide = times(mp[f, 1:13].reshape(12 * CY, CZ), pz[...])
+        for part in range(3):
+            rows = 4 * CY
+            fine[m, 4 * part : 4 * part + 4] = applied(py[...], wide[rows * part : rows * part + rows]).reshape(4, CY, CZ)
 
 
 def make_sources(fl, vyz, summed, src, plane, ry, rz):
@@ -213,8 +247,8 @@
         return 0
 
     lax.fori_loop(0, COARSE, pair, 0)
-    level = jnp.dot(summed[...].reshape(COARSE * CY, CZ), rz[...], precision=EXACT, preferred_element_type=F32)
-    level = jnp.dot(ry[...], level, precision=EXACT, preferred_element_type=F32).reshape(COARSE, CY, CZ)
+    level = times(summed[...].reshape(COARSE * CY, CZ), rz[...])
+    level = applied(ry[...], level).reshape(COARSE, CY, CZ)
     src[1:COARSE] = level[: COARSE - 1]
     plane[...] = level[COARSE - 1]
 
@@ -300,18 +334,22 @@
         send(trace.at[:, bottom], mp.at[pl.ds(TRACE, 6), high], down),
     ]
 
-    def same_block(shape):
-        return iota2(shape, 0) // CY == iota2(shape, 1) // CY
-
-    shape = (6 * CY, 6 * CY)
-    py[...] = jnp.where(same_block(shape), refine_weights(iota2(shape, 0) % CY, iota2(shape, 1) % CY, CY // 4), 0.0)
-    shape = (CZ, CZ)
-    pz[...] = refine_weights(iota2(shape, 1), iota2(shape, 0), CZ // 4)
-    rz[...] = jnp.where(CZ // 4 + iota2(shape, 0) // 2 == iota2(shape, 1), 0.125, 0.0).astype(F32)
-    shape = (COARSE * CY, COARSE * CY)
-    ry[...] = jnp.where(
-        same_block(shape) & (CY // 4 + iota2(shape, 1) % CY // 2 == iota2(shape, 0) % CY), 1.0, 0.0
-    ).astype(F32)
+    def fill(ref, weights, shape):
+        part = weights(iota2(shape, 0), iota2(shape, 1)).astype(jnp.bfloat16)
+        wide = ref.shape[1] != shape[1]
+        for k in range(3):
+            if wide:
+                ref[:, shape[1] * k : shape[1] * k + shape[1]] = part
+            else:
+                ref[shape[0] * k : shape[0] * k + shape[0], :] = part
+
+    def in_block(r, c, weights):
+        return jnp.where(r // CY == c // CY, weights, 0.0)
+
+    fill(rz, lambda r, c: jnp.where(CZ // 4 + r // 2 == c, 0.125, 0.0), (CZ, CZ))
+    fill(ry, lambda r, c: in_block(r, c, jnp.where(CY // 4 + c % CY // 2 == r % CY, 1.0, 0.0)), (COARSE * CY, COARSE * CY))
+    fill(pz, lambda r, c: refine_weights(c, r, CZ // 4), (CZ, CZ))
+    fill(py, lambda r, c: in_block(r, c, refine_weights(r % CY, c % CY, CY // 4)), (4 * CY, 4 * CY))
 
     for copy in loads[:6]:
         copy.wait()
@@ -362,24 +400,17 @@
 
     lax.fori_loop(3, FINE + 3, flux_own, 0)
 
-    def weno_inner(q, _):
-        weno(fpm, oh, 3, FINE - 5, q // 4, tile_at(q % 4))
-        return 0
-
-    lax.fori_loop(0, 20, weno_inner, 0)
-
     for copy in second:
         copy.wait_recv()
     for jj in range(3):
         split_flux(fl, fine, fpm, jj, blk != 0)
         split_flux(fl, fine, fpm, FINE + 3 + jj, blk != blocks - 1)
 
-    def weno_outer(q, _):
-        weno(fpm, oh, 0, 4, q // 4, tile_at(q % 4))
-        weno(fpm, oh, FINE - 3, 4, q // 4, tile_at(q % 4))
-        return 0
-
-    lax.fori_loop(0, 20, weno_outer, 0)
+    def faces(q, _):
+        weno(fpm, oh, q // 4, tile_at(q % 4))
+        return 0
+
+    lax.fori_loop(0, 20, faces, 0)
 
     for copy in third:
         copy.wait_recv()
@@ -415,10 +446,10 @@
             pltpu.VMEM((15, CY, CZ), F32),
             pltpu.VMEM((3, 12, CY, CZ), F32),
             pltpu.VMEM((10, FINE + 6, CY, CZ), F32),
-            pltpu.VMEM((6 * CY, 6 * CY), F32),
-            pltpu.VMEM((CZ, CZ), F32),
-            pltpu.VMEM((COARSE * CY, COARSE * CY), F32),
-            pltpu.VMEM((CZ, CZ), F32),
+            pltpu.VMEM((4 * CY, 3 * 4 * CY), jnp.bfloat16),
+            pltpu.VMEM((3 * CZ, CZ), jnp.bfloat16),
+            pltpu.VMEM((COARSE * CY, 3 * COARSE * CY), jnp.bfloat16),
+            pltpu.VMEM((3 * CZ, CZ), jnp.bfloat16),
             pltpu.SemaphoreType.DMA((12,)),
             pltpu.SemaphoreType.DMA((24,)),
             pltpu.SemaphoreType.DMA((24,)),

time: 26.1 us -> 24.3 us (0.931)
  Pallas kernels: 25.3 us -> 23.6 us
    pallas_call x1, Pallas kernels: 23.6 us -> 21.9 us  [on_device(): pl.pallas_call(functools.partial(kernel, sizes), out_shape=(pltpu.VMEM(me...]
where the time goes in v2:
time: 24.3 us; the launch traced here: 24.2 us
  Pallas kernels  23.6 us (97%)
  between operations  0.64 us (3%)
    pallas_call x1, Pallas kernels, on_device(): pl.pallas_call(functools.partial(kernel, sizes), out_shape=(pltpu.VMEM(me...  21.9 us
    pallas_call x1, Pallas kernels, on_device(): pl.pallas_call(write_out, out_shape=(jax.ShapeDtypeStruct(metric_out, F32...  1.72 us

profile of v2, /device:TPU:1, one launch (start us, length us, event | category | flops | bytes accessed | tf_op | source)
XLA Modules:
  0.0 24.2 jit_solution(7703331555483227524)
XLA Ops:
  0.6 21.9 %shard_map.122 = (f32[15,8,16,256]{3,2,1,0:T(8,128)S(1)}, f32[5,16,16,256]{3,2,1,0:T(8,128)S(1)}) custom-call(f32[8,16,256]{2,1,0:T(8,128)} %lapse.1, f32[8,16,256]{2,1,0:T(8,128)} %conf.1, f32[8,16,256]{2,1,0:T(8,128)} %curv.1, f32[6,8,16,256]{3,2,1,0:T(8,128)} %metric.1, f32[6,8,16,256]{3,2,1,0:T(8,128)} %trace.1, f32[3,8,16,256]{3,2,1,0:T(8,128)} %shift.1, ...), custom_call_target="tpu_custom_call" | custom-call | flops 60000000 | bytes 8000000 | tf_op jit(solution)/shard_map/pallas_call | solution.py:434
  22.5 1.7 %shard_map.123 = (f32[15,8,16,256]{3,2,1,0:T(8,128)}, f32[1,5,16,16,256]{4,3,2,1,0:T(8,128)}) custom-call(f32[15,8,16,256]{3,2,1,0:T(8,128)S(1)} %get-tuple-element.4.pb, f32[5,16,16,256]{3,2,1,0:T(8,128)S(1)} %get-tuple-element.5.ph), custom_call_target="tpu_custom_call" | custom-call | bytes 6400000 | tf_op jit(solution)/shard_map/pallas_call | solution.py:461

commit v3 on v2

--- a/solution.py
+++ b/solution.py
@@ -42,6 +42,17 @@
     return out
 
 
+def halves(v):
+    high = v.astype(jnp.bfloat16)
+    return [high, (v - high.astype(F32)).astype(jnp.bfloat16)]
+
+
+def stencil(to, source, n):
+    ahead = (source - to) & (n - 1)
+    near = jnp.where(ahead == 1, 8.0, jnp.where(ahead == n - 1, -8.0, 0.0))
+    return jnp.where(ahead == 2, -1.0, jnp.where(ahead == n - 2, 1.0, near))
+
+
 def first_of(moved):
     return (moved[0] - moved[3]) + 8.0 * (moved[2] - moved[1])
 
@@ -58,41 +69,50 @@
     return (mp[f, r - 2] - mp[f, r + 2]) + 8.0 * (mp[f, r + 1] - mp[f, r - 1])
 
 
-def derivatives(mp, ob, dd, i):
-    r = i + 2
-    by12 = mp[SHIFT + 1, r] * (1.0 / 12.0)
-    bz12 = mp[SHIFT + 2, r] * (1.0 / 12.0)
-    for f in range(2, SHIFT):
-        v = mp[f, r]
-        ob[f, i] = by12 * ring_first(v, 0) + bz12 * ring_first(v, 1)
-    bx12 = mp[SHIFT, r] * (1.0 / 12.0)
-    for f in (LAPSE, CONF):
-        v = mp[f, r]
-        along = x_first(mp, f, r)
+def derivatives(mp, ob, dd, src, ysten, zsten, start, inner):
+    fields = range(1, SHIFT + 3)
+    layers = [start, start + 1]
+    parts = [[halves(mp[f, i + 2]) for f in fields] for i in layers]
+    flat = jnp.concatenate([jnp.concatenate(p, 1) for layer in parts for p in layer], 0)
+    flat = jnp.dot(flat, zsten[...], preferred_element_type=F32)
+    for slot, i in enumerate(layers):
+        r = i + 2
+        bx12, by12, bz12 = [mp[SHIFT + k, r] * (1.0 / 12.0) for k in range(3)]
+        base = len(fields) * slot - 1
+        dz = {f: flat[CY * (base + f) : CY * (base + f + 1)] for f in fields}
+        dy = {f: jnp.dot(ysten[...], jnp.concatenate(parts[slot][f - 1], 0), preferred_element_type=F32) for f in fields}
+
+        v = mp[LAPSE, r]
+        along = x_first(mp, LAPSE, r)
         ys, zs = rolled(v, 0), rolled(v, 1)
-        dz = first_of(zs)
-        ob[f, i] = bx12 * along + by12 * first_of(ys) + bz12 * dz
-        if f == LAPSE:
-            dd[10] = ring_first(along, 0) * (1.0 / 144.0)
-            dd[11] = ring_first(along, 1) * (1.0 / 144.0)
-            dd[12] = second_of(v, ys) * (1.0 / 12.0)
-            dd[13] = ring_first(dz, 0) * (1.0 / 144.0)
-            dd[14] = second_of(v, zs) * (1.0 / 12.0)
-    v = mp[LAPSE, r]
-    dd[9] = (16.0 * (mp[LAPSE, r - 1] + mp[LAPSE, r + 1]) - (mp[LAPSE, r - 2] + mp[LAPSE, r + 2]) - 30.0 * v) * (1.0 / 12.0)
-    for k in range(3):
-        v = mp[SHIFT + k, r]
-        dd[k] = x_first(mp, SHIFT + k, r) * (1.0 / 12.0)
-        dd[3 + k] = ring_first(v, 0) * (1.0 / 12.0)
-        dd[6 + k] = ring_first(v, 1) * (1.0 / 12.0)
-
-
-def rates(mp, ob, dd, i, tile):
+        lapse_z = first_of(zs)
+        ob[LAPSE, i] = bx12 * along + by12 * first_of(ys) + bz12 * lapse_z
+        outer = (mp[LAPSE, r - 2] + mp[LAPSE, r + 2]) + 30.0 * v
+        dd[slot, 9] = (16.0 * (mp[LAPSE, r - 1] + mp[LAPSE, r + 1]) - outer) * (1.0 / 12.0)
+        dd[slot, 10] = ring_first(along, 0) * (1.0 / 144.0)
+        dd[slot, 11] = ring_first(along, 1) * (1.0 / 144.0)
+        dd[slot, 12] = second_of(v, ys) * (1.0 / 12.0)
+        dd[slot, 13] = ring_first(lapse_z, 0) * (1.0 / 144.0)
+        dd[slot, 14] = second_of(v, zs) * (1.0 / 12.0)
+        for f in range(1, SHIFT):
+            moved = by12 * dy[f] + bz12 * dz[f]
+            if inner or f == CONF:
+                moved = moved + bx12 * x_first(mp, f, r)
+            if inner and f == CURV:
+                moved = moved + (4.0 * math.pi) * v * src[i]
+            ob[f, i] = moved
+        for k in range(3):
+            dd[slot, k] = x_first(mp, SHIFT + k, r) * (1.0 / 12.0)
+            dd[slot, 3 + k] = dy[SHIFT + k] * (1.0 / 12.0)
+            dd[slot, 6 + k] = dz[SHIFT + k] * (1.0 / 12.0)
+
+
+def rates(mp, ob, dd, slot, i, tile):
     r = i + 2
     al, ch, kk = [mp[(f, r) + tile] for f in (LAPSE, CONF, CURV)]
     g = [mp[(METRIC + p, r) + tile] for p in range(6)]
-    ds = [[dd[(3 * k + j,) + tile] for j in range(3)] for k in range(3)]
-    hess = [dd[(9 + p,) + tile] for p in range(6)]
+    ds = [[dd[(slot, 3 * k + j) + tile] for j in range(3)] for k in range(3)]
+    hess = [dd[(slot, 9 + p) + tile] for p in range(6)]
     div = ds[0][0] + ds[1][1] + ds[2][2]
     tdiv = div * (2.0 / 3.0)
     a, b, c, d, e, f = g
@@ -125,19 +145,9 @@
         ob[(9 + p, i) + tile] = ob[(9 + p, i) + tile] + scale * cv[p] - al2 * product + moved_c - ch * hess[p] + chtr3 * g[p]
 
 
-def advect_x(mp, ob, src, i):
-    r = i + 2
-    bx12 = mp[SHIFT, r] * (1.0 / 12.0)
-    for f in range(2, SHIFT):
-        moved = bx12 * x_first(mp, f, r)
-        if f == CURV:
-            moved = moved + (4.0 * math.pi) * mp[LAPSE, r] * src[i]
-        ob[f, i] = ob[f, i] + moved
-
-
 def split_flux(fl, fine, fpm, jj, keep):
-    odd = jj % 2
-    t = (jj + 1) // 2
+    odd = jj & 1
+    t = (jj + 1) >> 1
     u = t + 1 - 2 * odd
     lapse, shift, conf = [0.75 * fine[m, t] + 0.25 * fine[m, u] for m in range(3)]
     vel, pres = fl[5, jj], fl[6, jj]
@@ -206,8 +216,8 @@
 
 
 def refine_weights(fine_pos, coarse_pos, start):
-    center = start + fine_pos // 2
-    side = center + 2 * (fine_pos % 2) - 1
+    center = start + (fine_pos >> 1)
+    side = center + 2 * (fine_pos & 1) - 1
     return jnp.where(coarse_pos == center, 0.75, jnp.where(coarse_pos == side, 0.25, 0.0)).astype(F32)
 
 
@@ -227,12 +237,14 @@
     return jnp.dot(weights, jnp.concatenate(thirds(v), 0), preferred_element_type=F32)
 
 
-def make_fine(mp, fine, py, pz):
+def make_fine(mp, fine, py, pz, layers):
     for m, f in enumerate((LAPSE, SHIFT, CONF)):
-        wide = times(mp[f, 1:13].reshape(12 * CY, CZ), pz[...])
-        for part in range(3):
-            rows = 4 * CY
-            fine[m, 4 * part : 4 * part + 4] = applied(py[...], wide[rows * part : rows * part + rows]).reshape(4, CY, CZ)
+        coarse = jnp.concatenate([mp[f, 1 + t] for t in layers], 0)
+        wide = times(coarse, pz[...])
+        for part in range(0, len(layers), 4):
+            block = applied(py[...], wide[CY * part : CY * (part + 4)])
+            for k in range(4):
+                fine[m, layers[part + k]] = block[CY * k : CY * (k + 1)]
 
 
 def make_sources(fl, vyz, summed, src, plane, ry, rz):
@@ -253,8 +265,8 @@
     plane[...] = level[COARSE - 1]
 
 
-def kernel(sizes, lapse, conf, curv, metric, trace, shift, dens, mom, ener, vel, pres, ob, oh,
-           mp, fl, vyz, src, plane, summed, dd, fine, fpm, py, pz, ry, rz, lsem, ssem, rsem):
+def kernel(sizes, lapse, conf, curv, metric, trace, shift, dens, mom, ener, vel, pres, ob, oh, mp, src,
+           fl, vyz, plane, summed, dd, fine, fpm, py, pz, ry, rz, ysten, zsten, lsem, ssem, rsem):
     stars, blocks = sizes
     count = stars * blocks
     blk = lax.axis_index("blk")
@@ -267,6 +279,43 @@
     barrier = pltpu.get_barrier_semaphore()
     for device in (up, down):
         pl.semaphore_signal(barrier, inc=1, device_id=device, device_id_type=MESH)
+
+    pl.semaphore_wait(barrier, 2)
+
+    sends = []
+
+    def send(source, target, device):
+        k = len(sends)
+        copy = pltpu.make_async_remote_copy(
+            src_ref=source, dst_ref=target, send_sem=ssem.at[k], recv_sem=rsem.at[k], device_id=device, device_id_type=MESH
+        )
+        copy.start()
+        sends.append(copy)
+        return copy
+
+    top, bottom = pl.ds(COARSE - 2, 2), pl.ds(0, 2)
+    low, high = pl.ds(0, 2), pl.ds(COARSE + 2, 2)
+    bottom3, high3 = pl.ds(0, 3), pl.ds(COARSE + 2, 3)
+    ftop, flow, fhigh = pl.ds(FINE - 3, 3), pl.ds(0, 3), pl.ds(FINE + 3, 2)
+    first = [
+        send(shift.at[:, top], mp.at[pl.ds(SHIFT, 3), low], up),
+        send(shift.at[0, bottom3], mp.at[SHIFT, high3], down),
+        send(shift.at[pl.ds(1, 2), bottom], mp.at[pl.ds(SHIFT + 1, 2), high], down),
+        send(lapse.at[top], mp.at[LAPSE, low], up),
+        send(lapse.at[bottom3], mp.at[LAPSE, high3], down),
+        send(conf.at[top], mp.at[CONF, low], up),
+        send(conf.at[bottom3], mp.at[CONF, high3], down),
+    ]
+    second = []
+    for source, target in (
+        (lambda s: dens.at[0, s], lambda s: fl.at[0, s]),
+        (lambda s: mom.at[0, :, s], lambda s: fl.at[pl.ds(1, 3), s]),
+        (lambda s: ener.at[0, s], lambda s: fl.at[4, s]),
+        (lambda s: vel.at[0, 0, s], lambda s: fl.at[5, s]),
+        (lambda s: pres.at[0, s], lambda s: fl.at[6, s]),
+    ):
+        second.append(send(source(ftop), target(flow), up))
+        second.append(send(source(bottom), target(fhigh), down))
 
     own = pl.ds(2, COARSE)
     fown = pl.ds(3, FINE)
@@ -289,43 +338,41 @@
     ]
     for copy in loads:
         copy.start()
-    pl.semaphore_wait(barrier, 2)
-
-    sends = []
-
-    def send(source, target, device):
-        k = len(sends)
-        copy = pltpu.make_async_remote_copy(
-            src_ref=source, dst_ref=target, send_sem=ssem.at[k], recv_sem=rsem.at[k], device_id=device, device_id_type=MESH
-        )
-        copy.start()
-        sends.append(copy)
-        return copy
-
-    top, bottom = pl.ds(COARSE - 2, 2), pl.ds(0, 2)
-    low, high = pl.ds(0, 2), pl.ds(COARSE + 2, 2)
-    high3 = pl.ds(COARSE + 2, 3)
-    ftop, flow, fhigh = pl.ds(FINE - 3, 3), pl.ds(0, 3), pl.ds(FINE + 3, 3)
-    first = [
-        send(shift.at[:, top], mp.at[pl.ds(SHIFT, 3), low], up),
-        send(shift.at[0, flow], mp.at[SHIFT, high3], down),
-        send(shift.at[pl.ds(1, 2), bottom], mp.at[pl.ds(SHIFT + 1, 2), high], down),
-        send(lapse.at[top], mp.at[LAPSE, low], up),
-        send(lapse.at[flow], mp.at[LAPSE, high3], down),
-        send(conf.at[top], mp.at[CONF, low], up),
-        send(conf.at[flow], mp.at[CONF, high3], down),
-    ]
-    second = []
-    for source, target in (
-        (lambda s: dens.at[0, s], lambda s: fl.at[0, s]),
-        (lambda s: mom.at[0, :, s], lambda s: fl.at[pl.ds(1, 3), s]),
-        (lambda s: ener.at[0, s], lambda s: fl.at[4, s]),
-        (lambda s: vel.at[0, 0, s], lambda s: fl.at[5, s]),
-        (lambda s: pres.at[0, s], lambda s: fl.at[6, s]),
-    ):
-        second.append(send(source(ftop), target(flow), up))
-        second.append(send(source(flow), target(fhigh), down))
+
+    def fill(ref, weights, shape, copies=3):
+        part = weights(iota2(shape, 0), iota2(shape, 1)).astype(jnp.bfloat16)
+        wide = ref.shape[1] != shape[1]
+        for k in range(copies):
+            if wide:
+                ref[:, shape[1] * k : shape[1] * k + shape[1]] = part
+            else:
+                ref[shape[0] * k : shape[0] * k + shape[0], :] = part
+
+    def in_block(r, c, weights):
+        return jnp.where((r ^ c) < CY, weights, 0.0)
+
+    fill(rz, lambda r, c: jnp.where(CZ // 4 + (r >> 1) == c, 0.125, 0.0), (CZ, CZ))
+    fill(ry, lambda r, c: in_block(r, c, jnp.where(CY // 4 + ((c & CY - 1) >> 1) == (r & CY - 1), 1.0, 0.0)), (COARSE * CY, COARSE * CY))
+    fill(zsten, lambda r, c: stencil(c, r, CZ), (CZ, CZ), 2)
+    fill(ysten, lambda r, c: stencil(r, c, CY), (CY, CY), 2)
+    fill(pz, lambda r, c: refine_weights(c, r, CZ // 4), (CZ, CZ))
+    fill(py, lambda r, c: in_block(r, c, refine_weights(r & CY - 1, c & CY - 1, CY // 4)), (4 * CY, 4 * CY))
+
+    for copy in loads[:6]:
+        copy.wait()
+    make_sources(fl, vyz, summed, src, plane, ry, rz)
+    for copy in loads[6:9]:
+        copy.wait()
+    make_fine(mp, fine, py, pz, tuple(range(1, 1 + COARSE)))
+
+    def flux_own(jj, _):
+        split_flux(fl, fine, fpm, jj, None)
+        return 0
+
+    lax.fori_loop(3, FINE, flux_own, 0)
+    second.append(send(fpm.at[pl.ds(5, 5), 5], fpm.at[pl.ds(5, 5), FINE + 5], down))
     third = [
+        send(plane, src.at[0], up),
         send(curv.at[top], mp.at[CURV, low], up),
         send(curv.at[bottom], mp.at[CURV, high], down),
         send(metric.at[:, top], mp.at[pl.ds(METRIC, 6), low], up),
@@ -333,96 +380,84 @@
         send(trace.at[:, top], mp.at[pl.ds(TRACE, 6), low], up),
         send(trace.at[:, bottom], mp.at[pl.ds(TRACE, 6), high], down),
     ]
-
-    def fill(ref, weights, shape):
-        part = weights(iota2(shape, 0), iota2(shape, 1)).astype(jnp.bfloat16)
-        wide = ref.shape[1] != shape[1]
-        for k in range(3):
-            if wide:
-                ref[:, shape[1] * k : shape[1] * k + shape[1]] = part
-            else:
-                ref[shape[0] * k : shape[0] * k + shape[0], :] = part
-
-    def in_block(r, c, weights):
-        return jnp.where(r // CY == c // CY, weights, 0.0)
-
-    fill(rz, lambda r, c: jnp.where(CZ // 4 + r // 2 == c, 0.125, 0.0), (CZ, CZ))
-    fill(ry, lambda r, c: in_block(r, c, jnp.where(CY // 4 + c % CY // 2 == r % CY, 1.0, 0.0)), (COARSE * CY, COARSE * CY))
-    fill(pz, lambda r, c: refine_weights(c, r, CZ // 4), (CZ, CZ))
-    fill(py, lambda r, c: in_block(r, c, refine_weights(r % CY, c % CY, CY // 4)), (4 * CY, 4 * CY))
-
-    for copy in loads[:6]:
+    for copy in loads[9:]:
         copy.wait()
-    make_sources(fl, vyz, summed, src, plane, ry, rz)
-    third.append(send(plane, src.at[0], up))
-    for copy in loads[6:]:
-        copy.wait()
-
-    tiles = [(pl.ds(8 * y, 8), pl.ds(LANES * z, LANES)) for y in range(CY // 8) for z in range(CZ // LANES)]
 
     def tile_at(t):
-        return (pl.ds(pl.multiple_of(t // 2 * 8, 8), 8), pl.ds(pl.multiple_of(t % 2 * LANES, LANES), LANES))
-
-    def metric_layer(i):
-        derivatives(mp, ob, dd, i)
-
-        def one(t, _):
-            rates(mp, ob, dd, i, tile_at(t))
+        return (pl.ds(pl.multiple_of((t >> 1) * 8, 8), 8), pl.ds(pl.multiple_of((t & 1) * LANES, LANES), LANES))
+
+    def metric_layers(start, inner):
+        derivatives(mp, ob, dd, src, ysten, zsten, start, inner)
+
+        def pair(q, _):
+            slot, y = q >> 1, q & 1
+            for z in range(CZ // LANES):
+                tile = (pl.ds(pl.multiple_of(8 * y, 8), 8), pl.ds(LANES * z, LANES))
+                rates(mp, ob, dd, slot, start + slot, tile)
             return 0
 
-        lax.fori_loop(0, len(tiles), one, 0)
-
-    def inner(i, _):
-        metric_layer(i)
-        advect_x(mp, ob, src, i)
+        lax.fori_loop(0, 4, pair, 0)
+
+    def inner(k, _):
+        metric_layers(2 + 2 * k, True)
         return 0
 
-    def edge(k):
-        return k + k // 2 * (COARSE - 4)
-
     def outer(k, _):
-        metric_layer(edge(k))
+        metric_layers(k * (COARSE - 2), False)
         return 0
 
-    def last(k, _):
-        advect_x(mp, ob, src, edge(k))
-        return 0
-
-    lax.fori_loop(2, COARSE - 2, inner, 0)
+    lax.fori_loop(0, COARSE // 2 - 2, inner, 0)
     for copy in first:
         copy.wait_recv()
-    lax.fori_loop(0, 4, outer, 0)
-    make_fine(mp, fine, py, pz)
-
-    def flux_own(jj, _):
+    lax.fori_loop(0, 2, outer, 0)
+    make_fine(mp, fine, py, pz, (0, 1 + COARSE, 2 + COARSE, 3 + COARSE))
+    for jj in range(FINE, FINE + 3):
         split_flux(fl, fine, fpm, jj, None)
-        return 0
-
-    lax.fori_loop(3, FINE + 3, flux_own, 0)
 
     for copy in second:
         copy.wait_recv()
     for jj in range(3):
         split_flux(fl, fine, fpm, jj, blk != 0)
-        split_flux(fl, fine, fpm, FINE + 3 + jj, blk != blocks - 1)
+    for jj in range(FINE + 3, FINE + 5):
+        split_flux(fl, fine, fpm, jj, blk != blocks - 1)
+    for n in range(5, 10):
+        fpm[n, FINE + 5] = jnp.where(blk != blocks - 1, fpm[n, FINE + 5], 0.0)
 
     def faces(q, _):
-        weno(fpm, oh, q // 4, tile_at(q % 4))
+        weno(fpm, oh, q >> 2, tile_at(q & 3))
         return 0
 
     lax.fori_loop(0, 20, faces, 0)
 
     for copy in third:
         copy.wait_recv()
-    lax.fori_loop(0, 4, last, 0)
     for copy in sends:
         copy.wait_send()
 
 
-def write_out(pb, ph, ob, oh, sem):
-    copies = [pltpu.make_async_copy(pb, ob, sem.at[0]), pltpu.make_async_copy(ph, oh.at[0], sem.at[1])]
-    for copy in copies:
+def write_out(pb, ph, mp, src, ob, oh, edge, sem):
+    copies = []
+
+    def put(source, target):
+        copy = pltpu.make_async_copy(source, target, sem.at[len(copies)])
         copy.start()
+        copies.append(copy)
+
+    rest = SHIFT - CURV
+    middle = pl.ds(2, COARSE - 4)
+    put(pb.at[pl.ds(CURV, rest), middle], ob.at[pl.ds(CURV, rest), middle])
+    put(ph, oh.at[0])
+    put(pb.at[pl.ds(0, CURV)], ob.at[pl.ds(0, CURV)])
+    for k, i in enumerate((0, 1, COARSE - 2, COARSE - 1)):
+        r = i + 2
+        bx12 = mp[SHIFT, r] * (1.0 / 12.0)
+        for f in range(CURV, SHIFT):
+            moved = bx12 * x_first(mp, f, r)
+            if f == CURV:
+                moved = moved + (4.0 * math.pi) * mp[LAPSE, r] * src[i]
+            edge[f - CURV, k] = pb[f, i] + moved
+        if k % 2:
+            put(edge.at[:, pl.ds(k - 1, 2)], ob.at[pl.ds(CURV, rest), pl.ds(i - 1, 2)])
     for copy in copies:
         copy.wait()
 
@@ -433,37 +468,42 @@
     metric_out, fluid_out = (15, COARSE, CY, CZ), (5, FINE, CY, CZ)
     part = pl.pallas_call(
         functools.partial(kernel, sizes),
-        out_shape=(pltpu.VMEM(metric_out, F32), pltpu.VMEM(fluid_out, F32)),
+        out_shape=(
+            pltpu.VMEM(metric_out, F32),
+            pltpu.VMEM(fluid_out, F32),
+            pltpu.VMEM((18, COARSE + 5, CY, CZ), F32),
+            pltpu.VMEM((COARSE, CY, CZ), F32),
+        ),
         in_specs=[hbm] * 11,
-        out_specs=(vmem, vmem),
+        out_specs=(vmem,) * 4,
         scratch_shapes=[
-            pltpu.VMEM((18, COARSE + 5, CY, CZ), F32),
             pltpu.VMEM((7, FINE + 6, CY, CZ), F32),
             pltpu.VMEM((2, FINE, CY, CZ), F32),
-            pltpu.VMEM((COARSE, CY, CZ), F32),
             pltpu.VMEM((CY, CZ), F32),
             pltpu.VMEM((COARSE, CY, CZ), F32),
-            pltpu.VMEM((15, CY, CZ), F32),
+            pltpu.VMEM((2, 15, CY, CZ), F32),
             pltpu.VMEM((3, 12, CY, CZ), F32),
             pltpu.VMEM((10, FINE + 6, CY, CZ), F32),
             pltpu.VMEM((4 * CY, 3 * 4 * CY), jnp.bfloat16),
             pltpu.VMEM((3 * CZ, CZ), jnp.bfloat16),
             pltpu.VMEM((COARSE * CY, 3 * COARSE * CY), jnp.bfloat16),
             pltpu.VMEM((3 * CZ, CZ), jnp.bfloat16),
+            pltpu.VMEM((CY, 2 * CY), jnp.bfloat16),
+            pltpu.VMEM((2 * CZ, CZ), jnp.bfloat16),
             pltpu.SemaphoreType.DMA((12,)),
-            pltpu.SemaphoreType.DMA((24,)),
-            pltpu.SemaphoreType.DMA((24,)),
+            pltpu.SemaphoreType.DMA((25,)),
+            pltpu.SemaphoreType.DMA((25,)),
         ],
-        compiler_params=pltpu.CompilerParams(collective_id=0, has_side_effects=True, vmem_limit_bytes=58 << 20),
+        compiler_params=pltpu.CompilerParams(collective_id=0, has_side_effects=True, vmem_limit_bytes=54 << 20),
         cost_estimate=pl.CostEstimate(flops=60_000_000, bytes_accessed=8_000_000, transcendentals=0),
     )(*arrays)
     anywhere = pl.BlockSpec(memory_space=pl.ANY)
     return pl.pallas_call(
         write_out,
         out_shape=(jax.ShapeDtypeStruct(metric_out, F32), jax.ShapeDtypeStruct((1,) + fluid_out, F32)),
-        in_specs=[vmem] * 2,
+        in_specs=[vmem] * 4,
         out_specs=(anywhere, anywhere),
-        scratch_shapes=[pltpu.SemaphoreType.DMA((2,))],
+        scratch_shapes=[pltpu.VMEM((SHIFT - CURV, 4, CY, CZ), F32), pltpu.SemaphoreType.DMA((5,))],
         compiler_params=pltpu.CompilerParams(vmem_limit_bytes=16 << 20),
         cost_estimate=pl.CostEstimate(flops=0, bytes_accessed=6_400_000, transcendentals=0),
     )(*part)

time: 24.3 us -> 23.8 us (0.979)
  the two profiles are of different devices: /device:TPU:1 before, /device:TPU:6 now
where the time goes in v3:
time: 23.8 us; the launch traced here: 23.5 us
  Pallas kernels  22.8 us (96%)
  between operations  0.64 us (3%)
    pallas_call x1, Pallas kernels, on_device(): pl.pallas_call(functools.partial(kernel, sizes), out_shape=(pltpu.VMEM(me...  21.1 us
    pallas_call x1, Pallas kernels, on_device(): pl.pallas_call(write_out, out_shape=(jax.ShapeDtypeStruct(metric_out, F32...  1.74 us

profile of v3, /device:TPU:6, one launch (start us, length us, event | category | flops | bytes accessed | tf_op | source)
XLA Modules:
  0.0 23.5 jit_solution(14059280891414149231)
XLA Ops:
  0.6 21.1 %shard_map.122 = (f32[15,8,16,256]{3,2,1,0:T(8,128)S(1)}, f32[5,16,16,256]{3,2,1,0:T(8,128)S(1)}, f32[18,13,16,256]{3,2,1,0:T(8,128)S(1)}, f32[8,16,256]{2,1,0:T(8,128)S(1)}) custom-call(f32[8,16,256]{2,1,0:T(8,128)} %lapse.1, f32[8,16,256]{2,1,0:T(8,128)} %conf.1, f32[8,16,256]{2,1,0:T(8,128)} %curv.1, f32[6,8,16,256]{3,2,1,0:T(8,128)} %metric.1, ...), custom_call_target="tpu_custom_call" | custom-call | flops 60000000 | bytes 8000000 | tf_op jit(solution)/shard_map/pallas_call | solution.py:469
  21.7 1.7 %shard_map.123 = (f32[15,8,16,256]{3,2,1,0:T(8,128)}, f32[1,5,16,16,256]{4,3,2,1,0:T(8,128)}) custom-call(f32[15,8,16,256]{3,2,1,0:T(8,128)S(1)} %get-tuple-element.6.pb, f32[5,16,16,256]{3,2,1,0:T(8,128)S(1)} %get-tuple-element.7.ph, f32[18,13,16,256]{3,2,1,0:T(8,128)S(1)} %get-tuple-element.8.mp, f32[8,16,256]{2,1,0:T(8,128)S(1)} %get-tuple-element.9.src), custom_call_target="tpu_custom_call" | custom-call | bytes 6400000 | tf_op jit(solution)/shard_map/pallas_call | solution.py:501

commit v4 on v3

--- a/solution.py
+++ b/solution.py
@@ -145,7 +145,7 @@
         ob[(9 + p, i) + tile] = ob[(9 + p, i) + tile] + scale * cv[p] - al2 * product + moved_c - ch * hess[p] + chtr3 * g[p]
 
 
-def split_flux(fl, fine, fpm, jj, keep):
+def split_flux(fl, fine, fpm, jj):
     odd = jj & 1
     t = (jj + 1) >> 1
     u = t + 1 - 2 * odd
@@ -164,8 +164,6 @@
         fp, fm = v * plus, v * minus
         if extra[n] is not None:
             fp, fm = fp + extra[n], fm + extra[n]
-        if keep is not None:
-            fp, fm = jnp.where(keep, fp, 0.0), jnp.where(keep, fm, 0.0)
         fpm[n, jj] = fp
         fpm[5 + n, jj] = fm
 
@@ -262,7 +260,7 @@
     level = times(summed[...].reshape(COARSE * CY, CZ), rz[...])
     level = applied(ry[...], level).reshape(COARSE, CY, CZ)
     src[1:COARSE] = level[: COARSE - 1]
-    plane[...] = level[COARSE - 1]
+    plane[...] = pltpu.roll(level[COARSE - 1], CZ - CZ // 4, 1)[CY // 4 : CY // 4 + CY // 2, : CZ // 2]
 
 
 def kernel(sizes, lapse, conf, curv, metric, trace, shift, dens, mom, ener, vel, pres, ob, oh, mp, src,
@@ -279,43 +277,6 @@
     barrier = pltpu.get_barrier_semaphore()
     for device in (up, down):
         pl.semaphore_signal(barrier, inc=1, device_id=device, device_id_type=MESH)
-
-    pl.semaphore_wait(barrier, 2)
-
-    sends = []
-
-    def send(source, target, device):
-        k = len(sends)
-        copy = pltpu.make_async_remote_copy(
-            src_ref=source, dst_ref=target, send_sem=ssem.at[k], recv_sem=rsem.at[k], device_id=device, device_id_type=MESH
-        )
-        copy.start()
-        sends.append(copy)
-        return copy
-
-    top, bottom = pl.ds(COARSE - 2, 2), pl.ds(0, 2)
-    low, high = pl.ds(0, 2), pl.ds(COARSE + 2, 2)
-    bottom3, high3 = pl.ds(0, 3), pl.ds(COARSE + 2, 3)
-    ftop, flow, fhigh = pl.ds(FINE - 3, 3), pl.ds(0, 3), pl.ds(FINE + 3, 2)
-    first = [
-        send(shift.at[:, top], mp.at[pl.ds(SHIFT, 3), low], up),
-        send(shift.at[0, bottom3], mp.at[SHIFT, high3], down),
-        send(shift.at[pl.ds(1, 2), bottom], mp.at[pl.ds(SHIFT + 1, 2), high], down),
-        send(lapse.at[top], mp.at[LAPSE, low], up),
-        send(lapse.at[bottom3], mp.at[LAPSE, high3], down),
-        send(conf.at[top], mp.at[CONF, low], up),
-        send(conf.at[bottom3], mp.at[CONF, high3], down),
-    ]
-    second = []
-    for source, target in (
-        (lambda s: dens.at[0, s], lambda s: fl.at[0, s]),
-        (lambda s: mom.at[0, :, s], lambda s: fl.at[pl.ds(1, 3), s]),
-        (lambda s: ener.at[0, s], lambda s: fl.at[4, s]),
-        (lambda s: vel.at[0, 0, s], lambda s: fl.at[5, s]),
-        (lambda s: pres.at[0, s], lambda s: fl.at[6, s]),
-    ):
-        second.append(send(source(ftop), target(flow), up))
-        second.append(send(source(bottom), target(fhigh), down))
 
     own = pl.ds(2, COARSE)
     fown = pl.ds(3, FINE)
@@ -336,43 +297,120 @@
             (trace, mp.at[pl.ds(TRACE, 6), own]),
         ))
     ]
-    for copy in loads:
-        copy.start()
-
-    def fill(ref, weights, shape, copies=3):
-        part = weights(iota2(shape, 0), iota2(shape, 1)).astype(jnp.bfloat16)
-        wide = ref.shape[1] != shape[1]
-        for k in range(copies):
-            if wide:
-                ref[:, shape[1] * k : shape[1] * k + shape[1]] = part
-            else:
-                ref[shape[0] * k : shape[0] * k + shape[0], :] = part
-
-    def in_block(r, c, weights):
-        return jnp.where((r ^ c) < CY, weights, 0.0)
-
-    fill(rz, lambda r, c: jnp.where(CZ // 4 + (r >> 1) == c, 0.125, 0.0), (CZ, CZ))
-    fill(ry, lambda r, c: in_block(r, c, jnp.where(CY // 4 + ((c & CY - 1) >> 1) == (r & CY - 1), 1.0, 0.0)), (COARSE * CY, COARSE * CY))
-    fill(zsten, lambda r, c: stencil(c, r, CZ), (CZ, CZ), 2)
-    fill(ysten, lambda r, c: stencil(r, c, CY), (CY, CY), 2)
-    fill(pz, lambda r, c: refine_weights(c, r, CZ // 4), (CZ, CZ))
-    fill(py, lambda r, c: in_block(r, c, refine_weights(r & CY - 1, c & CY - 1, CY // 4)), (4 * CY, 4 * CY))
-
-    for copy in loads[:6]:
-        copy.wait()
-    make_sources(fl, vyz, summed, src, plane, ry, rz)
-    for copy in loads[6:9]:
-        copy.wait()
-    make_fine(mp, fine, py, pz, tuple(range(1, 1 + COARSE)))
-
-    def flux_own(jj, _):
-        split_flux(fl, fine, fpm, jj, None)
+    def tile_at(t):
+        return (pl.ds(pl.multiple_of((t >> 1) * 8, 8), 8), pl.ds(pl.multiple_of((t & 1) * LANES, LANES), LANES))
+
+    def metric_layers(start, inner):
+        derivatives(mp, ob, dd, src, ysten, zsten, start, inner)
+
+        def pair(q, _):
+            slot, y = q >> 1, q & 1
+            for z in range(CZ // LANES):
+                tile = (pl.ds(pl.multiple_of(8 * y, 8), 8), pl.ds(LANES * z, LANES))
+                rates(mp, ob, dd, slot, start + slot, tile)
+            return 0
+
+        lax.fori_loop(0, 4, pair, 0)
+
+    def inner(k, _):
+        metric_layers(2 + 2 * k, True)
         return 0
 
-    lax.fori_loop(3, FINE, flux_own, 0)
-    second.append(send(fpm.at[pl.ds(5, 5), 5], fpm.at[pl.ds(5, 5), FINE + 5], down))
-    third = [
-        send(plane, src.at[0], up),
+    def first_part():
+        for copy in loads:
+            copy.start()
+
+        def fill(ref, weights, shape, copies=3):
+            part = weights(iota2(shape, 0), iota2(shape, 1)).astype(jnp.bfloat16)
+            wide = ref.shape[1] != shape[1]
+            for k in range(copies):
+                if wide:
+                    ref[:, shape[1] * k : shape[1] * k + shape[1]] = part
+                else:
+                    ref[shape[0] * k : shape[0] * k + shape[0], :] = part
+
+        def in_block(r, c, weights):
+            return jnp.where((r ^ c) < CY, weights, 0.0)
+
+        fill(rz, lambda r, c: jnp.where(CZ // 4 + (r >> 1) == c, 0.125, 0.0), (CZ, CZ))
+        fill(ry, lambda r, c: in_block(r, c, jnp.where(CY // 4 + ((c & CY - 1) >> 1) == (r & CY - 1), 1.0, 0.0)), (COARSE * CY, COARSE * CY))
+        fill(zsten, lambda r, c: stencil(c, r, CZ), (CZ, CZ), 2)
+        fill(ysten, lambda r, c: stencil(r, c, CY), (CY, CY), 2)
+        fill(pz, lambda r, c: refine_weights(c, r, CZ // 4), (CZ, CZ))
+        fill(py, lambda r, c: in_block(r, c, refine_weights(r & CY - 1, c & CY - 1, CY // 4)), (4 * CY, 4 * CY))
+
+        for copy in loads[:6]:
+            copy.wait()
+        make_sources(fl, vyz, summed, src, plane, ry, rz)
+        for copy in loads[6:9]:
+            copy.wait()
+        make_fine(mp, fine, py, pz, tuple(range(1, 1 + COARSE)))
+
+        def flux_own(jj, _):
+            split_flux(fl, fine, fpm, jj)
+            return 0
+
+        lax.fori_loop(3, FINE, flux_own, 0)
+
+    def second_part():
+        for copy in loads[9:]:
+            copy.wait()
+        lax.fori_loop(0, COARSE // 2 - 2, inner, 0)
+
+    early = lax.rem(me, max(2, count // 16)) == 0
+
+    @pl.when(early)
+    def _():
+        first_part()
+        second_part()
+
+    pl.semaphore_wait(barrier, 2)
+
+    sends = []
+
+    def send(source, target, device, when=None):
+        k = len(sends)
+        copy = pltpu.make_async_remote_copy(
+            src_ref=source, dst_ref=target, send_sem=ssem.at[k], recv_sem=rsem.at[k], device_id=device, device_id_type=MESH
+        )
+        sends.append(copy)
+        if when is None:
+            copy.start()
+        else:
+            pl.when(when)(copy.start)
+        return copy
+
+    starts, ends = blk == 0, blk == blocks - 1
+    continues_down, continues_up = jnp.logical_not(starts), jnp.logical_not(ends)
+
+    top, bottom = pl.ds(COARSE - 2, 2), pl.ds(0, 2)
+    low, high = pl.ds(0, 2), pl.ds(COARSE + 2, 2)
+    bottom3, high3 = pl.ds(0, 3), pl.ds(COARSE + 2, 3)
+    ftop, flow, fhigh = pl.ds(FINE - 3, 3), pl.ds(0, 3), pl.ds(FINE + 3, 2)
+    first = [
+        send(shift.at[:, top], mp.at[pl.ds(SHIFT, 3), low], up),
+        send(shift.at[0, bottom3], mp.at[SHIFT, high3], down),
+        send(shift.at[pl.ds(1, 2), bottom], mp.at[pl.ds(SHIFT + 1, 2), high], down),
+        send(lapse.at[top], mp.at[LAPSE, low], up),
+        send(lapse.at[bottom3], mp.at[LAPSE, high3], down),
+        send(conf.at[top], mp.at[CONF, low], up),
+        send(conf.at[bottom3], mp.at[CONF, high3], down),
+    ]
+    from_below, from_above = [], []
+    for source, target in (
+        (lambda s: dens.at[0, s], lambda s: fl.at[0, s]),
+        (lambda s: mom.at[0, :, s], lambda s: fl.at[pl.ds(1, 3), s]),
+        (lambda s: ener.at[0, s], lambda s: fl.at[4, s]),
+        (lambda s: vel.at[0, 0, s], lambda s: fl.at[5, s]),
+        (lambda s: pres.at[0, s], lambda s: fl.at[6, s]),
+    ):
+        from_below.append(send(source(ftop), target(flow), up, continues_up))
+        from_above.append(send(source(bottom), target(fhigh), down, continues_down))
+
+    pl.when(jnp.logical_not(early))(first_part)
+    from_above.append(send(fpm.at[pl.ds(5, 5), 5], fpm.at[pl.ds(5, 5), FINE + 5], down, continues_down))
+    third = [send(plane, src.at[0, pl.ds(0, CY // 2), pl.ds(0, CZ // 2)], up)]
+    third += [
         send(curv.at[top], mp.at[CURV, low], up),
         send(curv.at[bottom], mp.at[CURV, high], down),
         send(metric.at[:, top], mp.at[pl.ds(METRIC, 6), low], up),
@@ -380,48 +418,40 @@
         send(trace.at[:, top], mp.at[pl.ds(TRACE, 6), low], up),
         send(trace.at[:, bottom], mp.at[pl.ds(TRACE, 6), high], down),
     ]
-    for copy in loads[9:]:
-        copy.wait()
-
-    def tile_at(t):
-        return (pl.ds(pl.multiple_of((t >> 1) * 8, 8), 8), pl.ds(pl.multiple_of((t & 1) * LANES, LANES), LANES))
-
-    def metric_layers(start, inner):
-        derivatives(mp, ob, dd, src, ysten, zsten, start, inner)
-
-        def pair(q, _):
-            slot, y = q >> 1, q & 1
-            for z in range(CZ // LANES):
-                tile = (pl.ds(pl.multiple_of(8 * y, 8), 8), pl.ds(LANES * z, LANES))
-                rates(mp, ob, dd, slot, start + slot, tile)
-            return 0
-
-        lax.fori_loop(0, 4, pair, 0)
-
-    def inner(k, _):
-        metric_layers(2 + 2 * k, True)
-        return 0
+    pl.when(jnp.logical_not(early))(second_part)
 
     def outer(k, _):
         metric_layers(k * (COARSE - 2), False)
         return 0
 
-    lax.fori_loop(0, COARSE // 2 - 2, inner, 0)
     for copy in first:
         copy.wait_recv()
     lax.fori_loop(0, 2, outer, 0)
     make_fine(mp, fine, py, pz, (0, 1 + COARSE, 2 + COARSE, 3 + COARSE))
     for jj in range(FINE, FINE + 3):
-        split_flux(fl, fine, fpm, jj, None)
-
-    for copy in second:
-        copy.wait_recv()
-    for jj in range(3):
-        split_flux(fl, fine, fpm, jj, blk != 0)
-    for jj in range(FINE + 3, FINE + 5):
-        split_flux(fl, fine, fpm, jj, blk != blocks - 1)
-    for n in range(5, 10):
-        fpm[n, FINE + 5] = jnp.where(blk != blocks - 1, fpm[n, FINE + 5], 0.0)
+        split_flux(fl, fine, fpm, jj)
+
+    @pl.when(continues_down)
+    def _():
+        for copy in from_below:
+            copy.wait_recv()
+        for jj in range(3):
+            split_flux(fl, fine, fpm, jj)
+
+    @pl.when(starts)
+    def _():
+        fpm[:, :3] = jnp.zeros((10, 3, CY, CZ), F32)
+
+    @pl.when(continues_up)
+    def _():
+        for copy in from_above:
+            copy.wait_recv()
+        for jj in range(FINE + 3, FINE + 5):
+            split_flux(fl, fine, fpm, jj)
+
+    @pl.when(ends)
+    def _():
+        fpm[:, FINE + 3 :] = jnp.zeros((10, 3, CY, CZ), F32)
 
     def faces(q, _):
         weno(fpm, oh, q >> 2, tile_at(q & 3))
@@ -429,9 +459,22 @@
 
     lax.fori_loop(0, 20, faces, 0)
 
+    for copy in first:
+        copy.wait_send()
+
+    @pl.when(continues_up)
+    def _():
+        for copy in from_below:
+            copy.wait_send()
+
+    @pl.when(continues_down)
+    def _():
+        for copy in from_above:
+            copy.wait_send()
+
     for copy in third:
         copy.wait_recv()
-    for copy in sends:
+    for copy in third:
         copy.wait_send()
 
 
@@ -454,7 +497,12 @@
         for f in range(CURV, SHIFT):
             moved = bx12 * x_first(mp, f, r)
             if f == CURV:
-                moved = moved + (4.0 * math.pi) * mp[LAPSE, r] * src[i]
+                source = src[i]
+                if i == 0:
+                    source = jnp.concatenate([source[: CY // 2, : CZ // 2], jnp.zeros((CY // 2, CZ // 2), F32)], 1)
+                    around = jnp.zeros((CY // 4, CZ), F32)
+                    source = jnp.concatenate([around, pltpu.roll(source, CZ // 4, 1), around], 0)
+                moved = moved + (4.0 * math.pi) * mp[LAPSE, r] * source
             edge[f - CURV, k] = pb[f, i] + moved
         if k % 2:
             put(edge.at[:, pl.ds(k - 1, 2)], ob.at[pl.ds(CURV, rest), pl.ds(i - 1, 2)])
@@ -479,7 +527,7 @@
         scratch_shapes=[
             pltpu.VMEM((7, FINE + 6, CY, CZ), F32),
             pltpu.VMEM((2, FINE, CY, CZ), F32),
-            pltpu.VMEM((CY, CZ), F32),
+            pltpu.VMEM((CY // 2, CZ // 2), F32),
             pltpu.VMEM((COARSE, CY, CZ), F32),
             pltpu.VMEM((2, 15, CY, CZ), F32),
             pltpu.VMEM((3, 12, CY, CZ), F32),

time: 23.8 us -> 23.4 us (0.983)
  no operation moved by 1% of the time
where the time goes in v4:
time: 23.4 us; the launch traced here: 23.3 us
  Pallas kernels  22.7 us (97%)
  between operations  0.64 us (3%)
    pallas_call x1, Pallas kernels, on_device(): pl.pallas_call(functools.partial(kernel, sizes), out_shape=(pltpu.VMEM(me...  20.9 us
    pallas_call x1, Pallas kernels, on_device(): pl.pallas_call(write_out, out_shape=(jax.ShapeDtypeStruct(metric_out, F32...  1.74 us

profile of v4, /device:TPU:6, one launch (start us, length us, event | category | flops | bytes accessed | tf_op | source)
XLA Modules:
  0.0 23.3 jit_solution(2937268644571329754)
XLA Ops:
  0.6 20.9 %shard_map.122 = (f32[15,8,16,256]{3,2,1,0:T(8,128)S(1)}, f32[5,16,16,256]{3,2,1,0:T(8,128)S(1)}, f32[18,13,16,256]{3,2,1,0:T(8,128)S(1)}, f32[8,16,256]{2,1,0:T(8,128)S(1)}) custom-call(f32[8,16,256]{2,1,0:T(8,128)} %lapse.1, f32[8,16,256]{2,1,0:T(8,128)} %conf.1, f32[8,16,256]{2,1,0:T(8,128)} %curv.1, f32[6,8,16,256]{3,2,1,0:T(8,128)} %metric.1, ...), custom_call_target="tpu_custom_call" | custom-call | flops 60000000 | bytes 8000000 | tf_op jit(solution)/shard_map/pallas_call | solution.py:517
  21.6 1.7 %shard_map.123 = (f32[15,8,16,256]{3,2,1,0:T(8,128)}, f32[1,5,16,16,256]{4,3,2,1,0:T(8,128)}) custom-call(f32[15,8,16,256]{3,2,1,0:T(8,128)S(1)} %get-tuple-element.6.pb, f32[5,16,16,256]{3,2,1,0:T(8,128)S(1)} %get-tuple-element.7.ph, f32[18,13,16,256]{3,2,1,0:T(8,128)S(1)} %get-tuple-element.8.mp, f32[8,16,256]{2,1,0:T(8,128)S(1)} %get-tuple-element.9.src), custom_call_target="tpu_custom_call" | custom-call | bytes 6400000 | tf_op jit(solution)/shard_map/pallas_call | solution.py:549

commit v5 on v4

--- a/solution.py
+++ b/solution.py
@@ -145,16 +145,18 @@
         ob[(9 + p, i) + tile] = ob[(9 + p, i) + tile] + scale * cv[p] - al2 * product + moved_c - ch * hess[p] + chtr3 * g[p]
 
 
-def split_flux(fl, fine, fpm, jj):
+def motion(fl, fine, jj):
     odd = jj & 1
     t = (jj + 1) >> 1
     u = t + 1 - 2 * odd
     lapse, shift, conf = [0.75 * fine[m, t] + 0.25 * fine[m, u] for m in range(3)]
-    vel, pres = fl[5, jj], fl[6, jj]
     root = lax.rsqrt(conf)
-    weight = lapse * (root * root * root) * pres
-    moved = lapse * vel - shift
-    speed = lapse + jnp.abs(shift)
+    return lapse * fl[5, jj] - shift, lapse + jnp.abs(shift), lapse * (root * root * root) * fl[6, jj]
+
+
+def split_flux(fl, fine, fpm, jj, given=None):
+    moved, speed, weight = motion(fl, fine, jj) if given is None else given
+    vel = fl[5, jj]
     plus = 0.5 * (moved + speed)
     minus = 0.5 * (moved - speed)
     half = 0.5 * weight
@@ -264,7 +266,7 @@
 
 
 def kernel(sizes, lapse, conf, curv, metric, trace, shift, dens, mom, ener, vel, pres, ob, oh, mp, src,
-           fl, vyz, plane, summed, dd, fine, fpm, py, pz, ry, rz, ysten, zsten, lsem, ssem, rsem):
+           fl, vyz, plane, summed, dd, fine, fpm, py, pz, ry, rz, ysten, zsten, drift, lsem, ssem, rsem):
     stars, blocks = sizes
     count = stars * blocks
     blk = lax.axis_index("blk")
@@ -351,6 +353,8 @@
             return 0
 
         lax.fori_loop(3, FINE, flux_own, 0)
+        for k, value in enumerate(motion(fl, fine, 4)):
+            drift[0, k] = value
 
     def second_part():
         for copy in loads[9:]:
@@ -385,30 +389,33 @@
 
     top, bottom = pl.ds(COARSE - 2, 2), pl.ds(0, 2)
     low, high = pl.ds(0, 2), pl.ds(COARSE + 2, 2)
-    bottom3, high3 = pl.ds(0, 3), pl.ds(COARSE + 2, 3)
     ftop, flow, fhigh = pl.ds(FINE - 3, 3), pl.ds(0, 3), pl.ds(FINE + 3, 2)
     first = [
         send(shift.at[:, top], mp.at[pl.ds(SHIFT, 3), low], up),
-        send(shift.at[0, bottom3], mp.at[SHIFT, high3], down),
-        send(shift.at[pl.ds(1, 2), bottom], mp.at[pl.ds(SHIFT + 1, 2), high], down),
+        send(shift.at[:, bottom], mp.at[pl.ds(SHIFT, 3), high], down),
         send(lapse.at[top], mp.at[LAPSE, low], up),
-        send(lapse.at[bottom3], mp.at[LAPSE, high3], down),
+        send(lapse.at[bottom], mp.at[LAPSE, high], down),
         send(conf.at[top], mp.at[CONF, low], up),
-        send(conf.at[bottom3], mp.at[CONF, high3], down),
+        send(conf.at[bottom], mp.at[CONF, high], down),
     ]
     from_below, from_above = [], []
+    pressure = lambda s: pres.at[0, s]
     for source, target in (
         (lambda s: dens.at[0, s], lambda s: fl.at[0, s]),
         (lambda s: mom.at[0, :, s], lambda s: fl.at[pl.ds(1, 3), s]),
         (lambda s: ener.at[0, s], lambda s: fl.at[4, s]),
         (lambda s: vel.at[0, 0, s], lambda s: fl.at[5, s]),
-        (lambda s: pres.at[0, s], lambda s: fl.at[6, s]),
+        (pressure, lambda s: fl.at[6, s]),
     ):
         from_below.append(send(source(ftop), target(flow), up, continues_up))
-        from_above.append(send(source(bottom), target(fhigh), down, continues_down))
+        if source is pressure:
+            from_above.append(send(pres.at[0, pl.ds(0, 1)], fl.at[6, pl.ds(FINE + 3, 1)], down, continues_down))
+        else:
+            from_above.append(send(source(bottom), target(fhigh), down, continues_down))
 
     pl.when(jnp.logical_not(early))(first_part)
     from_above.append(send(fpm.at[pl.ds(5, 5), 5], fpm.at[pl.ds(5, 5), FINE + 5], down, continues_down))
+    from_above.append(send(drift.at[0], drift.at[1], down, continues_down))
     third = [send(plane, src.at[0, pl.ds(0, CY // 2), pl.ds(0, CZ // 2)], up)]
     third += [
         send(curv.at[top], mp.at[CURV, low], up),
@@ -427,7 +434,7 @@
     for copy in first:
         copy.wait_recv()
     lax.fori_loop(0, 2, outer, 0)
-    make_fine(mp, fine, py, pz, (0, 1 + COARSE, 2 + COARSE, 3 + COARSE))
+    make_fine(mp, fine, py, pz, (0, 1 + COARSE, 2 + COARSE, 2 + COARSE))
     for jj in range(FINE, FINE + 3):
         split_flux(fl, fine, fpm, jj)
 
@@ -446,8 +453,8 @@
     def _():
         for copy in from_above:
             copy.wait_recv()
-        for jj in range(FINE + 3, FINE + 5):
-            split_flux(fl, fine, fpm, jj)
+        split_flux(fl, fine, fpm, FINE + 3)
+        split_flux(fl, fine, fpm, FINE + 4, [drift[1, k] for k in range(3)])
 
     @pl.when(ends)
     def _():
@@ -519,7 +526,7 @@
         out_shape=(
             pltpu.VMEM(metric_out, F32),
             pltpu.VMEM(fluid_out, F32),
-            pltpu.VMEM((18, COARSE + 5, CY, CZ), F32),
+            pltpu.VMEM((18, COARSE + 4, CY, CZ), F32),
             pltpu.VMEM((COARSE, CY, CZ), F32),
         ),
         in_specs=[hbm] * 11,
@@ -538,6 +545,7 @@
             pltpu.VMEM((3 * CZ, CZ), jnp.bfloat16),
             pltpu.VMEM((CY, 2 * CY), jnp.bfloat16),
             pltpu.VMEM((2 * CZ, CZ), jnp.bfloat16),
+            pltpu.VMEM((2, 3, CY, CZ), F32),
             pltpu.SemaphoreType.DMA((12,)),
             pltpu.SemaphoreType.DMA((25,)),
             pltpu.SemaphoreType.DMA((25,)),

time: 23.4 us -> 23.4 us (level)
  no operation moved by 1% of the time
where the time goes in v5:
time: 23.4 us; the launch traced here: 23.3 us
  Pallas kernels  22.7 us (97%)
  between operations  0.64 us (3%)
    pallas_call x1, Pallas kernels, on_device(): pl.pallas_call(functools.partial(kernel, sizes), out_shape=(pltpu.VMEM(me...  20.9 us
    pallas_call x1, Pallas kernels, on_device(): pl.pallas_call(write_out, out_shape=(jax.ShapeDtypeStruct(metric_out, F32...  1.74 us

profile of v5, /device:TPU:6, one launch (start us, length us, event | category | flops | bytes accessed | tf_op | source)
XLA Modules:
  0.0 23.3 jit_solution(13620345179641804009)
XLA Ops:
  0.6 20.9 %shard_map.122 = (f32[15,8,16,256]{3,2,1,0:T(8,128)S(1)}, f32[5,16,16,256]{3,2,1,0:T(8,128)S(1)}, f32[18,12,16,256]{3,2,1,0:T(8,128)S(1)}, f32[8,16,256]{2,1,0:T(8,128)S(1)}) custom-call(f32[8,16,256]{2,1,0:T(8,128)} %lapse.1, f32[8,16,256]{2,1,0:T(8,128)} %conf.1, f32[8,16,256]{2,1,0:T(8,128)} %curv.1, f32[6,8,16,256]{3,2,1,0:T(8,128)} %metric.1, ...), custom_call_target="tpu_custom_call" | custom-call | flops 60000000 | bytes 8000000 | tf_op jit(solution)/shard_map/pallas_call | solution.py:524
  21.6 1.7 %shard_map.123 = (f32[15,8,16,256]{3,2,1,0:T(8,128)}, f32[1,5,16,16,256]{4,3,2,1,0:T(8,128)}) custom-call(f32[15,8,16,256]{3,2,1,0:T(8,128)S(1)} %get-tuple-element.6.pb, f32[5,16,16,256]{3,2,1,0:T(8,128)S(1)} %get-tuple-element.7.ph, f32[18,12,16,256]{3,2,1,0:T(8,128)S(1)} %get-tuple-element.8.mp, f32[8,16,256]{2,1,0:T(8,128)S(1)} %get-tuple-element.9.src), custom_call_target="tpu_custom_call" | custom-call | bytes 6400000 | tf_op jit(solution)/shard_map/pallas_call | solution.py:557

commit v6 on v5

--- a/solution.py
+++ b/solution.py
@@ -372,13 +372,20 @@
 
     sends = []
 
-    def send(source, target, device, when=None):
+    def send(source, target, device, when=None, loaded=None):
         k = len(sends)
-        copy = pltpu.make_async_remote_copy(
-            src_ref=source, dst_ref=target, send_sem=ssem.at[k], recv_sem=rsem.at[k], device_id=device, device_id_type=MESH
-        )
+
+        def copy_of(ref):
+            return pltpu.make_async_remote_copy(
+                src_ref=ref, dst_ref=target, send_sem=ssem.at[k], recv_sem=rsem.at[k], device_id=device, device_id_type=MESH
+            )
+
+        copy = copy_of(source)
         sends.append(copy)
-        if when is None:
+        if loaded is not None:
+            pl.when(early)(copy_of(loaded).start)
+            pl.when(jnp.logical_not(early))(copy.start)
+        elif when is None:
             copy.start()
         else:
             pl.when(when)(copy.start)
@@ -391,8 +398,8 @@
     low, high = pl.ds(0, 2), pl.ds(COARSE + 2, 2)
     ftop, flow, fhigh = pl.ds(FINE - 3, 3), pl.ds(0, 3), pl.ds(FINE + 3, 2)
     first = [
-        send(shift.at[:, top], mp.at[pl.ds(SHIFT, 3), low], up),
-        send(shift.at[:, bottom], mp.at[pl.ds(SHIFT, 3), high], down),
+        send(shift.at[:, top], mp.at[pl.ds(SHIFT, 3), low], up, loaded=mp.at[pl.ds(SHIFT, 3), pl.ds(COARSE, 2)]),
+        send(shift.at[:, bottom], mp.at[pl.ds(SHIFT, 3), high], down, loaded=mp.at[pl.ds(SHIFT, 3), pl.ds(2, 2)]),
         send(lapse.at[top], mp.at[LAPSE, low], up),
         send(lapse.at[bottom], mp.at[LAPSE, high], down),
         send(conf.at[top], mp.at[CONF, low], up),

time: 23.4 us -> 23.4 us (level)
  no operation moved by 1% of the time
where the time goes in v6:
time: 23.4 us; the launch traced here: 23.3 us
  Pallas kernels  22.7 us (97%)
  between operations  0.64 us (3%)
    pallas_call x1, Pallas kernels, on_device(): pl.pallas_call(functools.partial(kernel, sizes), out_shape=(pltpu.VMEM(me...  20.9 us
    pallas_call x1, Pallas kernels, on_device(): pl.pallas_call(write_out, out_shape=(jax.ShapeDtypeStruct(metric_out, F32...  1.74 us

profile of v6, /device:TPU:6, one launch (start us, length us, event | category | flops | bytes accessed | tf_op | source)
XLA Modules:
  0.0 23.3 jit_solution(11713197360961014303)
XLA Ops:
  0.6 20.9 %shard_map.122 = (f32[15,8,16,256]{3,2,1,0:T(8,128)S(1)}, f32[5,16,16,256]{3,2,1,0:T(8,128)S(1)}, f32[18,12,16,256]{3,2,1,0:T(8,128)S(1)}, f32[8,16,256]{2,1,0:T(8,128)S(1)}) custom-call(f32[8,16,256]{2,1,0:T(8,128)} %lapse.1, f32[8,16,256]{2,1,0:T(8,128)} %conf.1, f32[8,16,256]{2,1,0:T(8,128)} %curv.1, f32[6,8,16,256]{3,2,1,0:T(8,128)} %metric.1, ...), custom_call_target="tpu_custom_call" | custom-call | flops 60000000 | bytes 8000000 | tf_op jit(solution)/shard_map/pallas_call | solution.py:531
  21.6 1.7 %shard_map.123 = (f32[15,8,16,256]{3,2,1,0:T(8,128)}, f32[1,5,16,16,256]{4,3,2,1,0:T(8,128)}) custom-call(f32[15,8,16,256]{3,2,1,0:T(8,128)S(1)} %get-tuple-element.6.pb, f32[5,16,16,256]{3,2,1,0:T(8,128)S(1)} %get-tuple-element.7.ph, f32[18,12,16,256]{3,2,1,0:T(8,128)S(1)} %get-tuple-element.8.mp, f32[8,16,256]{2,1,0:T(8,128)S(1)} %get-tuple-element.9.src), custom_call_target="tpu_custom_call" | custom-call | bytes 6400000 | tf_op jit(solution)/shard_map/pallas_call | solution.py:564
